TPU v7x, 128 devices: a whole 4x4x4 slice. The times are simulated.
128 devices in a mesh: rep: 16 (over y, x_hi, core), tp: 8 (over z, x_lo).
Axes of the slice: x: 4 (x_hi: 2, x_lo: 2; x = x_hi * 2 + x_lo), y: 4, z: 4, core: 2. Of those that a mesh axis runs over, the one named last changes fastest.
Arguments:
- latent_cache: bfloat16 [16, 8192, 576], P('rep', 'tp'), may hold values from -8 to 8
- query_nope: bfloat16 [384, 16384], P('rep', 'tp'), may hold values from -6 to 6
- query_rope: bfloat16 [384, 8192], P('rep', 'tp'), may hold values from -7 to 7
- new_latent: bfloat16 [384, 576], P('rep'), may hold values from -8 to 8
- key_up: bfloat16 [128, 128, 512], P('tp'), may hold values from -0.5 to 0.5
- value_up: bfloat16 [128, 512, 128], P('tp'), may hold values from -0.75 to 0.75
- prompt_owner: int32 [16], replicated, may hold values from 0 to 15, each once
- prompt_length: int32 [16], replicated, may hold values from 1024 to 8192, as said below
- sample_prompt: int32 [384, 1], P('rep'), may hold values from 0 to 15; in each aligned block of 24 rows (0 to 23, 24 to 47, ...) at most 3 rows name the same one
Outputs:
- head_output: bfloat16 [384, 16384], P('rep', 'tp')
Inputs may be any that keep to these rules, and one draw needn't show every extreme that they name: `sample_prompt`: the rows of one replica group, 24 of them, name no prompt more than 3 times, a bound that some block reaches. `prompt_length`: one prompt has all 8192 positions live and one has 1024.
All inputs are finite; a program needn't handle non-finite values.
Results may differ from a plain program's by a relative error of at most 0.0073.
Values may be sent and summed in bfloat16 or wider, within the bound.
A program may use at most 128 MiB of HBM per device.

v0:
```python
import jax
import jax.numpy as jnp
from jax import lax
from jax.sharding import PartitionSpec as P

big_negative = -1e30


def slot_tables(sample_prompt, prompt_owner, prompt_length, capacity):
    samples = sample_prompt.shape[0]
    slot_count = prompt_owner.shape[0]
    labels = sample_prompt[:, 0]
    slot_iota = jnp.arange(slot_count, dtype=jnp.int32)
    prompt_hits = labels[:, None] == slot_iota[None, :]
    slot_of = jnp.sum(jnp.where(prompt_hits, prompt_owner[None, :], 0), axis=1)
    owner_hits = prompt_owner[:, None] == slot_iota[None, :]
    slot_length = jnp.sum(jnp.where(owner_hits, prompt_length[:, None], 0), axis=0)
    matches = slot_of[None, :] == slot_iota[:, None]
    ranking = jnp.cumsum(matches.astype(jnp.int32), axis=1) - 1
    wanted = matches[:, None, :] & (
        ranking[:, None, :] == jnp.arange(capacity, dtype=jnp.int32)[None, :, None]
    )
    sample_ids = jnp.arange(samples, dtype=jnp.int32)
    members = jnp.min(jnp.where(wanted, sample_ids[None, None, :], samples), axis=2)
    return (members, slot_length)


def absorb(query_nope, query_rope, key_up):
    samples = query_nope.shape[0]
    head_count, nope_width, latent_width = key_up.shape
    nope_part = query_nope.reshape(samples, head_count, nope_width)
    rope_part = query_rope.reshape(samples, head_count, -1)
    latent_query = jnp.einsum("shn,hnl->shl", nope_part, key_up, preferred_element_type=jnp.float32)
    scaling = (nope_width + rope_part.shape[2]) ** (-0.5)
    joined = jnp.concatenate([latent_query, rope_part.astype(jnp.float32)], axis=2) * scaling
    return joined.astype(jnp.bfloat16)


def local_scores(queries, prefix_keys, live_count):
    scores = jnp.einsum("rk,nk->rn", queries, prefix_keys, preferred_element_type=jnp.float32)
    position = jnp.arange(prefix_keys.shape[0], dtype=jnp.int32)
    return jnp.where(position[None, :] < live_count, scores, big_negative)


def weighted_sums(scores, row_top, prefix_keys, latent_width):
    weights = jnp.exp(scores - row_top[:, None])
    totals = jnp.sum(weights, axis=1)
    numerator = jnp.dot(
        weights.astype(jnp.bfloat16),
        prefix_keys[:, :latent_width],
        preferred_element_type=jnp.float32,
    )
    return (numerator, totals)


def finish(numerator, totals, row_top, own_score, fresh_latent, value_up):
    own_weight = jnp.exp(own_score - row_top)
    latent_width = numerator.shape[-1]
    numerator = numerator + own_weight[..., None] * fresh_latent[:, None, :latent_width].astype(
        jnp.float32
    )
    latent_out = (numerator / (totals + own_weight)[..., None]).astype(jnp.bfloat16)
    values = jnp.einsum("shl,hlv->shv", latent_out, value_up, preferred_element_type=jnp.float32)
    return values.astype(jnp.bfloat16).reshape(values.shape[0], -1)


def shards(
    latent_cache,
    query_nope,
    query_rope,
    new_latent,
    key_up,
    value_up,
    prompt_owner,
    prompt_length,
    sample_prompt,
):
    query_own = absorb(query_nope, query_rope, key_up)
    group_samples = sample_prompt.shape[0]
    capacity_rows = max(2, 2 * group_samples // lax.axis_size("rep"))
    members, slot_length = slot_tables(sample_prompt, prompt_owner, prompt_length, capacity_rows)
    shard_width = latent_cache.shape[1]
    tp_rank = lax.axis_index("tp")
    live_all = jnp.clip(slot_length - tp_rank * shard_width, 0, shard_width)
    local_heads = key_up.shape[0]
    latent_width = value_up.shape[1]
    first_head = tp_rank * local_heads
    query_all = lax.all_gather(query_own, "tp", axis=1, tiled=True)
    own_all = jnp.einsum("shk,sk->sh", query_all, new_latent, preferred_element_type=jnp.float32)
    prefixes = lax.all_gather(latent_cache, "rep", axis=0, tiled=True)
    samples, head_count, key_width = query_all.shape

    def one_slot(slot_index, carried):
        numer_acc, totals_acc, top_acc = carried
        prefix_keys = lax.dynamic_index_in_dim(prefixes, slot_index, 0, keepdims=False)
        member_rows = lax.dynamic_index_in_dim(members, slot_index, 0, keepdims=False)
        capacity = member_rows.shape[0]
        queries = jnp.take(query_all, member_rows, axis=0, mode="fill", fill_value=0)
        own_score = jnp.take(own_all, member_rows, axis=0, mode="fill", fill_value=0.0)
        scores = local_scores(queries.reshape(-1, key_width), prefix_keys, live_all[slot_index])
        local_top = jnp.maximum(jnp.max(scores, axis=1), own_score.reshape(-1))
        row_top = lax.pmax(local_top, "tp")
        numerator, totals = weighted_sums(scores, row_top, prefix_keys, latent_width)
        numer_acc = numer_acc.at[member_rows].add(
            numerator.reshape(capacity, head_count, latent_width), mode="drop"
        )
        totals_acc = totals_acc.at[member_rows].add(
            totals.reshape(capacity, head_count), mode="drop"
        )
        top_acc = top_acc.at[member_rows].add(row_top.reshape(capacity, head_count), mode="drop")
        return (numer_acc, totals_acc, top_acc)

    initial = (
        jnp.zeros((samples, head_count, latent_width), jnp.float32),
        jnp.zeros((samples, head_count), jnp.float32),
        jnp.zeros((samples, head_count), jnp.float32),
    )
    numer_acc, totals_acc, top_acc = lax.fori_loop(0, members.shape[0], one_slot, initial)
    numer_own, totals_own = (
        lax.psum_scatter(numer_acc, "tp", scatter_dimension=1, tiled=True),
        lax.psum_scatter(totals_acc, "tp", scatter_dimension=1, tiled=True),
    )
    top_own = lax.dynamic_slice_in_dim(top_acc, first_head, local_heads, 1)
    own_part = lax.dynamic_slice_in_dim(own_all, first_head, local_heads, 1)
    return finish(numer_own, totals_own, top_own, own_part, new_latent, value_up)


def solution(mesh):
    return jax.shard_map(
        shards,
        mesh=mesh,
        in_specs=(
            P("rep", "tp", None),
            P("rep", "tp"),
            P("rep", "tp"),
            P("rep", None),
            P("tp", None, None),
            P("tp", None, None),
            P(),
            P(),
            P("rep", None),
        ),
        out_specs=P("rep", "tp"),
        check_vma=False,
    )
```

profile of v0, /device:TPU:1, one launch (start us, length us, event | category | flops | bytes accessed | tf_op | source)
XLA Modules:
  0.0 960.5 jit_solution(1569264634689293652)
XLA Ops:
  11.8 87.8 %all-gather.3.cloned.1.call-done = bf16[24,128,576]{2,0,1:T(8,128)(2,1)} async-done(((bf16[24,16,576]{2,0,1:T(8,128)(2,1)}), bf16[24,128,576]{2,0,1:T(8,128)(2,1)}) %all-gather.3.cloned.1.call-update) | async-done | bytes 3538960 | tf_op jit(solution)/shard_map/all_gather | solution.py:88
  99.7 4.8 copy.29
  105.8 115.4 %all-gather.5.cloned.1.call-done = bf16[16,1024,576]{1,2,0:T(8,128)(2,1)} async-done(((bf16[1,1024,576]{1,2,0:T(8,128)(2,1)}), bf16[16,1024,576]{1,2,0:T(8,128)(2,1)}) %all-gather.5.cloned.1.call-update) | async-done | bytes 18874384 | tf_op jit(solution)/shard_map/all_gather | solution.py:90
  221.3 3.4 broadcast_in_dim.118
  224.7 501.3 %while.17 = (s32[]{:T(128)}, f32[24,128,512]{2,1,0:T(8,128)}, f32[24,128]{1,0:T(8,128)S(1)}, f32[24,128]{1,0:T(8,128)S(1)}, s32[16,3]{1,0:T(8,128)S(1)}, /*index...) while((s32[]{:T(128)}, f32[24,128,512]{2,1,0:T(8,128)}, ...), condition=%wide.region_11.12_spmd, body=%wide.region_4.11_spmd.sunk | while | flops 858418304 | bytes 17074916 | solution.py:118
  232.9 15.2 %pmax.12 = f32[384]{0:T(512)S(1)} all-reduce(f32[384]{0:T(512)S(1)} %bitcast_maximum_fusion.2), channel_id=1, replica_groups=mesh['rep'=16,'tp'=8] {'tp'}, use_global_device_ids=true, to_apply=%region_6.6 | all-reduce | flops 384 | bytes 3072 | tf_op jit(solution)/shard_map/while/body/eval_jaxpr/pmax | solution.py:102
  266.0 12.5 %pmax.12 = f32[384]{0:T(512)S(1)} all-reduce(f32[384]{0:T(512)S(1)} %bitcast_maximum_fusion.2), channel_id=1, replica_groups=mesh['rep'=16,'tp'=8] {'tp'}, use_global_device_ids=true, to_apply=%region_6.6 | all-reduce | flops 384 | bytes 3072 | tf_op jit(solution)/shard_map/while/body/eval_jaxpr/pmax | solution.py:102
  296.5 14.2 %pmax.12 = f32[384]{0:T(512)S(1)} all-reduce(f32[384]{0:T(512)S(1)} %bitcast_maximum_fusion.2), channel_id=1, replica_groups=mesh['rep'=16,'tp'=8] {'tp'}, use_global_device_ids=true, to_apply=%region_6.6 | all-reduce | flops 384 | bytes 3072 | tf_op jit(solution)/shard_map/while/body/eval_jaxpr/pmax | solution.py:102
  328.5 12.5 %pmax.12 = f32[384]{0:T(512)S(1)} all-reduce(f32[384]{0:T(512)S(1)} %bitcast_maximum_fusion.2), channel_id=1, replica_groups=mesh['rep'=16,'tp'=8] {'tp'}, use_global_device_ids=true, to_apply=%region_6.6 | all-reduce | flops 384 | bytes 3072 | tf_op jit(solution)/shard_map/while/body/eval_jaxpr/pmax | solution.py:102
  347.9 2.9 scatter_fusion
  359.1 14.0 %pmax.12 = f32[384]{0:T(512)S(1)} all-reduce(f32[384]{0:T(512)S(1)} %bitcast_maximum_fusion.2), channel_id=1, replica_groups=mesh['rep'=16,'tp'=8] {'tp'}, use_global_device_ids=true, to_apply=%region_6.6 | all-reduce | flops 384 | bytes 3072 | tf_op jit(solution)/shard_map/while/body/eval_jaxpr/pmax | solution.py:102
  391.0 12.6 %pmax.12 = f32[384]{0:T(512)S(1)} all-reduce(f32[384]{0:T(512)S(1)} %bitcast_maximum_fusion.2), channel_id=1, replica_groups=mesh['rep'=16,'tp'=8] {'tp'}, use_global_device_ids=true, to_apply=%region_6.6 | all-reduce | flops 384 | bytes 3072 | tf_op jit(solution)/shard_map/while/body/eval_jaxpr/pmax | solution.py:102
  421.4 14.0 %pmax.12 = f32[384]{0:T(512)S(1)} all-reduce(f32[384]{0:T(512)S(1)} %bitcast_maximum_fusion.2), channel_id=1, replica_groups=mesh['rep'=16,'tp'=8] {'tp'}, use_global_device_ids=true, to_apply=%region_6.6 | all-reduce | flops 384 | bytes 3072 | tf_op jit(solution)/shard_map/while/body/eval_jaxpr/pmax | solution.py:102
  453.4 12.8 %pmax.12 = f32[384]{0:T(512)S(1)} all-reduce(f32[384]{0:T(512)S(1)} %bitcast_maximum_fusion.2), channel_id=1, replica_groups=mesh['rep'=16,'tp'=8] {'tp'}, use_global_device_ids=true, to_apply=%region_6.6 | all-reduce | flops 384 | bytes 3072 | tf_op jit(solution)/shard_map/while/body/eval_jaxpr/pmax | solution.py:102
  484.1 13.8 %pmax.12 = f32[384]{0:T(512)S(1)} all-reduce(f32[384]{0:T(512)S(1)} %bitcast_maximum_fusion.2), channel_id=1, replica_groups=mesh['rep'=16,'tp'=8] {'tp'}, use_global_device_ids=true, to_apply=%region_6.6 | all-reduce | flops 384 | bytes 3072 | tf_op jit(solution)/shard_map/while/body/eval_jaxpr/pmax | solution.py:102
  515.8 13.0 %pmax.12 = f32[384]{0:T(512)S(1)} all-reduce(f32[384]{0:T(512)S(1)} %bitcast_maximum_fusion.2), channel_id=1, replica_groups=mesh['rep'=16,'tp'=8] {'tp'}, use_global_device_ids=true, to_apply=%region_6.6 | all-reduce | flops 384 | bytes 3072 | tf_op jit(solution)/shard_map/while/body/eval_jaxpr/pmax | solution.py:102
  546.7 13.5 %pmax.12 = f32[384]{0:T(512)S(1)} all-reduce(f32[384]{0:T(512)S(1)} %bitcast_maximum_fusion.2), channel_id=1, replica_groups=mesh['rep'=16,'tp'=8] {'tp'}, use_global_device_ids=true, to_apply=%region_6.6 | all-reduce | flops 384 | bytes 3072 | tf_op jit(solution)/shard_map/while/body/eval_jaxpr/pmax | solution.py:102
  578.2 13.3 %pmax.12 = f32[384]{0:T(512)S(1)} all-reduce(f32[384]{0:T(512)S(1)} %bitcast_maximum_fusion.2), channel_id=1, replica_groups=mesh['rep'=16,'tp'=8] {'tp'}, use_global_device_ids=true, to_apply=%region_6.6 | all-reduce | flops 384 | bytes 3072 | tf_op jit(solution)/shard_map/while/body/eval_jaxpr/pmax | solution.py:102
  609.4 13.4 %pmax.12 = f32[384]{0:T(512)S(1)} all-reduce(f32[384]{0:T(512)S(1)} %bitcast_maximum_fusion.2), channel_id=1, replica_groups=mesh['rep'=16,'tp'=8] {'tp'}, use_global_device_ids=true, to_apply=%region_6.6 | all-reduce | flops 384 | bytes 3072 | tf_op jit(solution)/shard_map/while/body/eval_jaxpr/pmax | solution.py:102
  640.8 13.1 %pmax.12 = f32[384]{0:T(512)S(1)} all-reduce(f32[384]{0:T(512)S(1)} %bitcast_maximum_fusion.2), channel_id=1, replica_groups=mesh['rep'=16,'tp'=8] {'tp'}, use_global_device_ids=true, to_apply=%region_6.6 | all-reduce | flops 384 | bytes 3072 | tf_op jit(solution)/shard_map/while/body/eval_jaxpr/pmax | solution.py:102
  671.8 13.4 %pmax.12 = f32[384]{0:T(512)S(1)} all-reduce(f32[384]{0:T(512)S(1)} %bitcast_maximum_fusion.2), channel_id=1, replica_groups=mesh['rep'=16,'tp'=8] {'tp'}, use_global_device_ids=true, to_apply=%region_6.6 | all-reduce | flops 384 | bytes 3072 | tf_op jit(solution)/shard_map/while/body/eval_jaxpr/pmax | solution.py:102
  703.2 13.1 %pmax.12 = f32[384]{0:T(512)S(1)} all-reduce(f32[384]{0:T(512)S(1)} %bitcast_maximum_fusion.2), channel_id=1, replica_groups=mesh['rep'=16,'tp'=8] {'tp'}, use_global_device_ids=true, to_apply=%region_6.6 | all-reduce | flops 384 | bytes 3072 | tf_op jit(solution)/shard_map/while/body/eval_jaxpr/pmax | solution.py:102
  727.3 86.2 %reduce-scatter.7.cloned.1.call-done = f32[16,24]{1,0:T(8,128)} async-done(((f32[128,24]{1,0:T(8,128)}), f32[16,24]{1,0:T(8,128)}) %reduce-scatter.7.cloned.1.call-update) | async-done | bytes 1552
  814.3 135.4 %reduce-scatter.5.cloned.1.call-done = f32[24,16,512]{2,1,0:T(8,128)} async-done(((f32[24,128,512]{2,1,0:T(8,128)}), f32[24,16,512]{2,1,0:T(8,128)}) %reduce-scatter.5.cloned.1.call-update) | async-done | bytes 786448 | tf_op jit(solution)/shard_map/reduce_scatter | solution.py:120
  (313 shorter events, 295.8 us)
Async XLA Ops:
  6.5 1.6 copy-start
  6.5 93.1 %all-gather.3.cloned.1.call-start = ((), (), s32[]{:S(2)}) async-start(), calls=%async_computation.2 | async-start | bytes 4423680 | tf_op jit(solution)/shard_map/all_gather | solution.py:88
  9.4 1.7 copy-start.3
  9.4 1.7 copy-start.4
  9.4 2.3 copy-start.5
  10.4 210.9 %all-gather.5.cloned.1.call-start = ((), (), s32[]{:S(2)}) async-start(), calls=%async_computation.3 | async-start | bytes 20054016 | tf_op jit(solution)/shard_map/all_gather | solution.py:90
  11.1 802.4 %reduce-scatter.7.cloned.1.call-start = ((), (), s32[]{:S(2)}) async-start(), calls=%async_computation.5 | async-start | bytes 73728
  11.8 92.7 %copy-start.2 = (bf16[24,576]{1,0:T(8,128)(2,1)S(1)}, bf16[24,576]{1,0:T(8,128)(2,1)}, u32[]{:S(2)}) copy-start(bf16[24,576]{1,0:T(8,128)(2,1)} %param.14) | copy-start | bytes 82948
  99.7 4.8 copy-start.1
  726.7 223.0 %reduce-scatter.5.cloned.1.call-start = ((), (), s32[]{:S(2)}) async-start(), calls=%async_computation.4 | async-start | bytes 7077888 | tf_op jit(solution)/shard_map/reduce_scatter | solution.py:120
Sparse Core Ops, SparseCore 0:
  10.5 89.1 all-gather.2
  102.1 119.0 all-gather.4
  726.9 86.5 reduce-scatter.6
  815.9 133.8 reduce-scatter.4
where the time goes:
time: 964 us; the launch traced here: 960 us
  waiting for transfers between devices  426 us (44%)
  blocking collectives  214 us (22%)
  local copies, waits for them, and re-layouts  120 us (12%)
  other arithmetic  111 us (12%)
  matrix products  74.5 us (8%)
  between operations  13.2 us (1%)
    pmax x16, blocking collectives, one_slot(): row_top = lax.pmax(local_top, 'tp')  214 us
    reduce_scatter x1, waiting for transfers between devices, shards(): lax.psum_scatter(numer_acc, 'tp', scatter_dimension=1, tiled=True)  135 us
    all_gather x1, waiting for transfers between devices, shards(): prefixes = lax.all_gather(latent_cache, 'rep', axis=0, tiled=True)  115 us
    all_gather x1, waiting for transfers between devices, shards(): query_all = lax.all_gather(query_own, 'tp', axis=1, tiled=True)  87.8 us
    unnamed x5, waiting for transfers between devices  87.4 us
    scatter-add x16, other arithmetic, one_slot(): numer_acc.at[member_rows]  45.4 us
    dynamic_slice x32, local copies, waits for them, and re-layouts, one_slot(): lax.dynamic_index_in_dim(prefixes, slot_index, 0, keepdims=False)  45 us
    gather x16, local copies, waits for them, and re-layouts, one_slot(): jnp.take(query_all, member_rows, axis=0, mode='fill', fill_value=0)  44 us
  transfers between devices with their start and end apart: 4, of which 4 were waited for; matrix products, arithmetic and copies ran while one was open for 1% of the time, Pallas kernels for 0%

commit v1 on v0

v1 whole, which is shorter than its diff:
```python
import functools

import jax
import jax.numpy as jnp
from jax import lax
from jax.experimental import pallas as pl
from jax.experimental.pallas import tpu as pltpu
from jax.sharding import PartitionSpec as P

MESH = pl.DeviceIdType.MESH
NEG = -1e30
F32, BF16 = jnp.float32, jnp.bfloat16

S, HL, SLOTS, CAP = 24, 16, 16, 3
PL = SLOTS * CAP
ROWS = PL * HL
LAT, ROPE, NOPE, DV = 512, 64, 128, 128
QW = LAT + 2 * ROPE
SHARD, CH = 1024, 512
PK = CH + CH * ROPE // LAT
RB = 256


def dot(a, b):
    return jnp.dot(a, b, preferred_element_type=F32)


def dot_nt(a, b):
    return lax.dot_general(a, b, (((1,), (1,)), ((), ())), preferred_element_type=F32)


def block(i):
    return pl.ds(pl.multiple_of(i * (CAP * HL), 16), CAP * HL)


def iota(shape, dim):
    return lax.broadcasted_iota(jnp.int32, shape, dim)


def kernel(
    latent, nope_h, rope_h, new_h, ku_h, vu_h, owner, length, labels, out,
    nope, rope, new, ku, vu, rtmp, kv, stage, qsend, q, qhi, mtop, tot, acc, osend, orecv,
    lsem, qss, qrs, kss, krs, vss, vrs, oss, ors,
):
    r, t = lax.axis_index("rep"), lax.axis_index("tp")
    y, xh, c, z, xl = r // 4, (r // 2) % 2, r % 2, t // 2, t % 2
    role_a = c == xl

    def dev(yy, xx, zz, cc):
        return ((yy * 2 + xx // 2) * 2 + cc, zz * 2 + xx % 2)

    x = xh * 2 + xl
    zp, zm = dev(y, x, (z + 1) % 4, c), dev(y, x, (z + 3) % 4, c)
    sib = dev(y, x, z, 1 - c)
    partner = dev(y, xh * 2 + 1 - xl, z, 1 - c)
    slot = (y * 2 + xh) * 2 + xl

    base = jnp.where(role_a, 0, 16)
    loads = [
        pltpu.make_async_copy(nope_h, nope, lsem.at[0]),
        pltpu.make_async_copy(rope_h, rope, lsem.at[1]),
        pltpu.make_async_copy(new_h, new, lsem.at[2]),
        pltpu.make_async_copy(ku_h, ku, lsem.at[3]),
        pltpu.make_async_copy(latent.at[0, :, pl.ds(LAT, ROPE)], rtmp, lsem.at[4]),
        pltpu.make_async_copy(latent.at[0, pl.ds(0, CH), pl.ds(0, LAT)], kv.at[base, pl.ds(0, CH)], lsem.at[5]),
        pltpu.make_async_copy(latent.at[0, pl.ds(CH, CH), pl.ds(0, LAT)], kv.at[base + 1, pl.ds(0, CH)], lsem.at[6]),
    ]
    for load in loads:
        load.start()
    vload = pltpu.make_async_copy(vu_h, vu, lsem.at[7])
    pl.when(role_a)(vload.start)

    barrier = pltpu.get_barrier_semaphore()

    def greet_core(i, _):
        @pl.when(jnp.logical_not(jnp.logical_and(role_a, i == y * 4 + x)))
        def _():
            pl.semaphore_signal(barrier, inc=1, device_id=dev(i // 4, i % 4, z, xl), device_id_type=MESH)
        return 0

    def greet_col(i, _):
        pl.semaphore_signal(barrier, inc=1, device_id=dev(i // 2, (i % 2) * 2 + c, z, 1 - xl), device_id_type=MESH)
        return 0

    for d in (zp, zm):
        pl.semaphore_signal(barrier, inc=1, device_id=d, device_id_type=MESH)
    lax.fori_loop(0, 16, greet_core, 0)
    lax.fori_loop(0, 8, greet_col, 0)

    for i in (4, 5, 6):
        loads[i].wait()
    spread = iota((ROPE, 2 * ROPE), 0) - iota((ROPE, 2 * ROPE), 1)
    lo_e, hi_e = (spread == 0).astype(BF16), (spread == -ROPE).astype(BF16)
    half = CH // 2
    for k in range(2):
        packed = dot(rtmp[pl.ds(k * CH, half), :], lo_e) + dot(rtmp[pl.ds(k * CH + half, half), :], hi_e)
        packed = packed.astype(BF16)
        for j in range(4):
            kv[base + k, pl.ds(CH, PK - CH), pl.ds(128 * j, 128)] = packed[64 * j : 64 * j + 64]

    lab = labels[...]
    sub, lane = iota((S, S), 0), iota((S, S), 1)
    lab_row = jnp.sum(jnp.where(sub == lane, lab.astype(F32), 0.0), axis=0, keepdims=True).astype(jnp.int32)
    same = lab == lab_row
    rank_row = jnp.sum(jnp.where(same & (sub < lane), 1.0, 0.0), axis=0, keepdims=True).astype(jnp.int32)
    rank_col = jnp.sum(jnp.where(same & (lane < sub), 1.0, 0.0), axis=1, keepdims=True).astype(jnp.int32)
    slot_row, slot_col = jnp.zeros_like(lab_row), jnp.zeros_like(lab)
    live = jnp.int32(0)
    for p in range(SLOTS):
        own = owner[p]
        slot_row = jnp.where(lab_row == p, own, slot_row)
        slot_col = jnp.where(lab == p, own, slot_col)
        live = live + jnp.where(own == slot, length[p], 0)
    place = (iota((PL, S), 0) == slot_row * CAP + rank_row).astype(BF16)
    unplace = (iota((S, PL), 1) == slot_col * CAP + rank_col).astype(BF16)

    for i in (0, 1, 2, 3):
        loads[i].wait()
    scale = (NOPE + ROPE) ** -0.5
    nope_s = dot(place, nope[...]).astype(BF16)
    rope_s = dot(place, rope[...]) * scale
    new_s = dot(place, new[...])
    new_s = jnp.concatenate([new_s[:, :LAT], jnp.concatenate([new_s[:, LAT:], jnp.zeros((PL, ROPE), F32)], axis=1)], axis=1)
    low = iota((PL, 2 * ROPE), 1) < ROPE
    for h in range(HL):
        rows = pl.ds(h, PL, stride=HL)
        lat_q = dot(nope_s[:, NOPE * h : NOPE * (h + 1)], ku[h]) * scale
        for j in range(4):
            stage[j, rows, :] = lat_q[:, 128 * j : 128 * j + 128]
        b = 128 * (h // 2)
        mine = rope_s[:, b : b + 128]
        if h % 2:
            mine = pltpu.roll(mine, ROPE, 1)
        if h < 9:
            piece = new_s[:, b : b + 128]
            if h % 2 == 0:
                piece = pltpu.roll(piece, ROPE, 1)
        else:
            piece = jnp.zeros_like(mine)
        stage[4, rows, :] = jnp.where(low, mine, piece)
    for j in range(5):
        qsend[:, pl.ds(128 * j, 128)] = stage[j].astype(BF16)

    def q_copy(s, d):
        return pltpu.make_async_remote_copy(
            src_ref=qsend.at[block(s)], dst_ref=q.at[block(r)], send_sem=qss.at[s], recv_sem=qrs.at[r], device_id=d, device_id_type=MESH
        )

    def q_dev(s):
        return dev(s // 4, ((s // 2) % 2) * 2 + s % 2, z, xl)

    own_q = pltpu.make_async_copy(qsend.at[block(r)], q.at[block(r)], qrs.at[r])

    def kv_copy(src, dst, sem, d):
        return pltpu.make_async_remote_copy(
            src_ref=kv.at[src], dst_ref=kv.at[dst], send_sem=kss.at[sem], recv_sem=krs.at[dst], device_id=d, device_id_type=MESH
        )

    o = jnp.where(role_a, 0, 8)

    def ring_own(k):
        return [kv_copy(o + k, o + 2 + k, k, zp), kv_copy(o + k, o + 4 + k, 2 + k, zm), kv_copy(o + k, o + k, 8 + k, sib)]

    def ring_pass(k):
        out_ = [kv_copy(o + k, o + k, 8 + k, sib)]
        if k == 2:
            out_.insert(0, kv_copy(o + 2, o + 6, 4, zp))
        if k == 5:
            out_.insert(0, kv_copy(o + 5, o + 7, 5, zm))
        return out_

    def arrived(k):
        kv_copy(k, k, 0, sib).wait_recv()

    def ring_step(k):
        arrived(o + k)
        for cp in ring_pass(k):
            cp.start()

    cross = [kv_copy(16 + k, 8 + k, 16 + k, partner) for k in range(2)]

    pl.semaphore_wait(barrier, jnp.where(role_a, 25, 26))

    @pl.when(role_a)
    def _():
        for k in range(2):
            for cp in ring_own(k):
                cp.start()

    def q_send(i, _):
        s = (slot + i) % SLOTS

        @pl.when(jnp.logical_and(role_a, i == 0))
        def _():
            own_q.start()

        @pl.when(jnp.logical_not(jnp.logical_and(role_a, i == 0)))
        def _():
            q_copy(s, q_dev(s)).start()
        return 0

    lax.fori_loop(0, SLOTS, q_send, 0)

    @pl.when(jnp.logical_not(role_a))
    def _():
        for cp in cross:
            cp.start()

    @pl.when(role_a)
    def _():
        for k in (2, 4, 3, 5):
            ring_step(k)

    @pl.when(jnp.logical_not(role_a))
    def _():
        arrived(8)
        for cp in ring_own(0):
            cp.start()

    def q_wait(i, _):
        g = (r + i) % SLOTS

        @pl.when(jnp.logical_and(role_a, i == 0))
        def _():
            own_q.wait()

        @pl.when(jnp.logical_not(jnp.logical_and(role_a, i == 0)))
        def _():
            pltpu.make_async_remote_copy(
                src_ref=qsend.at[block(0)], dst_ref=q.at[block(g)], send_sem=qss.at[0], recv_sem=qrs.at[g], device_id=sib, device_id_type=MESH
            ).wait_recv()
        return 0

    lax.fori_loop(0, SLOTS, q_wait, 0)

    halves = [
        pltpu.make_async_remote_copy(
            src_ref=vu_h.at[pl.ds(8 * k, 8)], dst_ref=vu.at[pl.ds(8 * k, 8)], send_sem=vss.at[k], recv_sem=vrs.at[k],
            device_id=dev(y, (xh if k == 0 else 1 - xh) * 2 + 1 - xl, z, c), device_id_type=MESH,
        )
        for k in range(2)
    ]

    @pl.when(role_a)
    def _():
        for cp in halves:
            cp.start()

    q3 = q[...]
    tail = q3[:, LAT:].astype(F32)
    wide_low = iota((ROWS, 2 * ROPE), 1) < ROPE
    stage[0] = tail
    tail = jnp.where(wide_low, tail, 0.0)
    qhi[...] = pltpu.roll(tail, ROPE, 1).astype(BF16)
    pieces = [stage[0, pl.ds(k, PL, stride=HL), :] for k in range(9)]
    new_p = []
    for k in range(5):
        left = pltpu.roll(pieces[2 * k], ROPE, 1)
        new_p.append(jnp.where(low, left, pieces[2 * k + 1] if k < 4 else 0.0))
    new_p = jnp.concatenate(new_p, axis=1).astype(BF16)
    by_row = (iota((ROWS, PL), 0) // HL == iota((ROWS, PL), 1)).astype(BF16)
    own_keys = dot(by_row, new_p)
    own_score = jnp.sum(q3[:, :LAT].astype(F32) * own_keys[:, :LAT], axis=1, keepdims=True)
    own_score = own_score + jnp.sum(tail * own_keys[:, LAT:], axis=1, keepdims=True)
    for j in range(4):
        acc[j] = own_keys[:, 128 * j : 128 * j + 128]
    mtop[...] = jnp.broadcast_to(own_score, mtop.shape)
    tot[...] = jnp.ones_like(tot)
    q[:, pl.ds(LAT, 2 * ROPE)] = tail.astype(BF16)

    def attend(ci):
        place_z = (ci % 8) // 2
        zz = (z + jnp.where(place_z == 1, 3, jnp.where(place_z == 2, 1, jnp.where(place_z == 3, 2, 0)))) % 4
        first = (zz * 2 + jnp.where(ci < 8, xl, 1 - xl)) * SHARD + (ci % 2) * CH
        keys = kv[ci, pl.ds(0, CH), :]
        rot = kv[ci, pl.ds(CH, PK - CH), :]
        rot = jnp.concatenate([rot[:, 128 * j : 128 * j + 128] for j in range(4)], axis=0)
        k_lo = jnp.concatenate([keys[:half], rot], axis=1)
        k_hi = jnp.concatenate([keys[half:], rot], axis=1)
        bias = jnp.where(first + iota((1, CH), 1) < live, 0.0, NEG)
        for b in range(ROWS // RB):
            rs = pl.ds(b * RB, RB)
            s_lo = dot_nt(q[rs, :], k_lo)
            s_hi = dot_nt(jnp.concatenate([q[rs, pl.ds(0, LAT)], qhi[rs, :]], axis=1), k_hi)
            s = jnp.concatenate([s_lo, s_hi], axis=1) + bias
            top = mtop[rs, pl.ds(0, 1)]
            new_top = jnp.maximum(top, jnp.max(s, axis=1, keepdims=True))
            shrink = jnp.exp(top - new_top)
            w = jnp.exp(s - new_top)
            tot[rs, :] = jnp.broadcast_to(tot[rs, pl.ds(0, 1)] * shrink + jnp.sum(w, axis=1, keepdims=True), (RB, 128))
            mtop[rs, :] = jnp.broadcast_to(new_top, (RB, 128))
            new = dot(w.astype(BF16), keys)
            for j in range(4):
                acc[j, rs, :] = acc[j, rs, :] * shrink + new[:, 128 * j : 128 * j + 128]

    def step(i, _):
        ci = i + (i % 8 == 3).astype(jnp.int32) - (i % 8 == 4).astype(jnp.int32)

        @pl.when(role_a)
        def _():
            for at, k in ((5, 6), (6, 7)):
                pl.when(i == at)(functools.partial(ring_step, k))
            pl.when(i >= 8)(lambda: arrived(ci))

        @pl.when(jnp.logical_not(role_a))
        def _():
            pl.when(i < 8)(lambda: arrived(ci))

            @pl.when(i == 2)
            def _():
                arrived(9)
                for cp in ring_own(1):
                    cp.start()

            for at, k in ((9, 2), (10, 4), (11, 3), (12, 5), (13, 6), (14, 7)):
                pl.when(i == at)(functools.partial(ring_step, k))

        attend(ci)
        return 0

    lax.fori_loop(0, 16, step, 0)

    @pl.when(role_a)
    def _():
        vload.wait()

    @pl.when(jnp.logical_not(role_a))
    def _():
        for cp in halves:
            cp.wait_recv()

    for h in range(HL):
        rows = pl.ds(h, PL, stride=HL)
        total = tot[rows, :]
        mean = jnp.concatenate([acc[j, rows, :] / total for j in range(4)], axis=1).astype(BF16)
        stage[0, rows, :] = dot(mean, vu[h])
    osend[...] = stage[0].astype(BF16)

    def o_copy(g):
        return pltpu.make_async_remote_copy(
            src_ref=osend.at[block(g)], dst_ref=orecv.at[block(slot)], send_sem=oss.at[g], recv_sem=ors.at[slot],
            device_id=(g, z * 2 + c), device_id_type=MESH,
        )

    own_o = pltpu.make_async_copy(osend.at[block(r)], orecv.at[block(r)], ors.at[r])

    def o_send(i, _):
        g = (r + i) % SLOTS
        kept = jnp.logical_and(role_a, i == 0)
        pl.when(kept)(own_o.start)
        pl.when(jnp.logical_not(kept))(lambda: o_copy(g).start())
        return 0

    lax.fori_loop(0, SLOTS, o_send, 0)

    @pl.when(role_a)
    def _():
        for cp in halves:
            cp.wait_send()

    @pl.when(jnp.logical_not(role_a))
    def _():
        for cp in cross:
            cp.wait_send()

    for k in range(2):
        for cp in ring_own(k):
            cp.wait_send()
    for k in range(2, 8):
        for cp in ring_pass(k):
            cp.wait_send()

    def all_wait(i, _):
        s = (slot + i) % SLOTS
        g = (r + i) % SLOTS
        kept = jnp.logical_and(role_a, i == 0)

        @pl.when(kept)
        def _():
            own_o.wait()

        @pl.when(jnp.logical_not(kept))
        def _():
            q_copy(s, sib).wait_send()
            o_copy(g).wait_send()
            pltpu.make_async_remote_copy(
                src_ref=osend.at[block(0)], dst_ref=orecv.at[block(s)], send_sem=oss.at[0], recv_sem=ors.at[s],
                device_id=sib, device_id_type=MESH,
            ).wait_recv()
        return 0

    lax.fori_loop(0, SLOTS, all_wait, 0)
    stage[0] = orecv[...].astype(F32)
    for h in range(HL):
        picked = stage[0, pl.ds(h, PL, stride=HL), :].astype(BF16)
        out[:, pl.ds(DV * h, DV)] = dot(unplace, picked).astype(BF16)


def shards(latent_cache, query_nope, query_rope, new_latent, key_up, value_up, prompt_owner, prompt_length, sample_prompt):
    hbm, smem, vmem = (pl.BlockSpec(memory_space=m) for m in (pl.ANY, pltpu.SMEM, pltpu.VMEM))
    dma = pltpu.SemaphoreType.DMA
    return pl.pallas_call(
        kernel,
        out_shape=jax.ShapeDtypeStruct(query_nope.shape, BF16),
        in_specs=[hbm] * 6 + [smem] * 2 + [vmem],
        out_specs=vmem,
        scratch_shapes=[
            pltpu.VMEM(query_nope.shape, BF16),
            pltpu.VMEM(query_rope.shape, BF16),
            pltpu.VMEM(new_latent.shape, BF16),
            pltpu.VMEM(key_up.shape, BF16),
            pltpu.VMEM(value_up.shape, BF16),
            pltpu.VMEM((SHARD, ROPE), BF16),
            pltpu.VMEM((18, PK, LAT), BF16),
            pltpu.VMEM((5, ROWS, 128), F32),
            pltpu.VMEM((ROWS, QW), BF16),
            pltpu.VMEM((ROWS, QW), BF16),
            pltpu.VMEM((ROWS, 2 * ROPE), BF16),
            pltpu.VMEM((ROWS, 128), F32),
            pltpu.VMEM((ROWS, 128), F32),
            pltpu.VMEM((4, ROWS, 128), F32),
            pltpu.VMEM((ROWS, DV), BF16),
            pltpu.VMEM((ROWS, DV), BF16),
            dma((8,)), dma((SLOTS,)), dma((SLOTS,)), dma((18,)), dma((16,)),
            dma((2,)), dma((2,)), dma((SLOTS,)), dma((SLOTS,)),
        ],
        compiler_params=pltpu.CompilerParams(collective_id=0, has_side_effects=True, vmem_limit_bytes=56 << 20),
        cost_estimate=pl.CostEstimate(flops=16 << 30, bytes_accessed=8 << 20, transcendentals=8 << 20),
    )(latent_cache, query_nope, query_rope, new_latent, key_up, value_up, prompt_owner, prompt_length, sample_prompt)


def solution(mesh):
    return jax.shard_map(
        shards,
        mesh=mesh,
        in_specs=(
            P("rep", "tp", None),
            P("rep", "tp"),
            P("rep", "tp"),
            P("rep", None),
            P("tp", None, None),
            P("tp", None, None),
            P(),
            P(),
            P("rep", None),
        ),
        out_specs=P("rep", "tp"),
        check_vma=False,
    )
```

time: 964 us -> 93.3 us (0.10)
  waiting for transfers between devices: 426 us -> 0 us
  blocking collectives: 214 us -> 0 us
  local copies, waits for them, and re-layouts: 120 us -> 5.29 us
  other arithmetic: 111 us -> 0 us
  Pallas kernels: 0 us -> 87.5 us
  matrix products: 74.5 us -> 0 us
  between operations: 13.2 us -> 0.01 us
    pmax x16 -> x0, blocking collectives: 214 us -> none  [one_slot(): row_top = lax.pmax(local_top, 'tp')]
    all_gather x2 -> x0, waiting for transfers between devices: 203 us -> none  [the longest x1 115 us: shards(): prefixes = lax.all_gather(latent_cache, 'rep', axis=0, tiled=True)]
    reduce_scatter x1 -> x0, waiting for transfers between devices: 135 us -> none  [shards(): lax.psum_scatter(numer_acc, 'tp', scatter_dimension=1, tiled=True)]
    pallas_call x0 -> x1, Pallas kernels: none -> 87.5 us  [shards(): pl.pallas_call(kernel, out_shape=jax.ShapeDtypeStruct(query_nope.shape, B...]
    unnamed x5 -> x0, waiting for transfers between devices: 87.4 us -> none
    dot_general x35 -> x0, matrix products: 74.5 us -> none  [the longest x16 37.2 us: weighted_sums(): jnp.dot(weights.astype(jnp.bfloat16), prefix_keys[:, :latent_width], pref...]
    scatter-add x48 -> x0, other arithmetic: 65.1 us -> none  [the longest x16 45.4 us: one_slot(): numer_acc.at[member_rows]]
    dynamic_slice x48 -> x0, local copies, waits for them, and re-layouts: 55.4 us -> none  [the longest x32 45 us: one_slot(): lax.dynamic_index_in_dim(prefixes, slot_index, 0, keepdims=False)]
  transfers between devices with their start and end apart: 4 -> 0, of which waited for: 4 -> 0; matrix products, arithmetic and copies ran while one was open for 1% -> 0% of each run, Pallas kernels for 0% -> 0%
where the time goes in v1:
time: 93.3 us; the launch traced here: 92.8 us
  Pallas kernels  87.5 us (94%)
  local copies, waits for them, and re-layouts  5.29 us (6%)
    pallas_call x1, Pallas kernels, shards(): pl.pallas_call(kernel, out_shape=jax.ShapeDtypeStruct(query_nope.shape, B...  87.5 us
    unnamed x3, local copies, waits for them, and re-layouts  5.29 us

profile of v1, /device:TPU:1, one launch (start us, length us, event | category | flops | bytes accessed | tf_op | source)
XLA Modules:
  0.0 92.8 jit_solution(3489758061115607003)
XLA Ops:
  0.0 1.3 %copy.11.labels = s32[24,1]{1,0:T(8,128)} copy(s32[24,1]{0,1:T(1,128)} %param.17) | data formatting | bytes 192 | tf_op args[8]
  1.3 2.4 %copy.10.latent = bf16[1,1024,576]{2,1,0:T(8,128)(2,1)} copy(bf16[1,1024,576]{1,2,0:T(8,128)(2,1)} %param.9) | data formatting | bytes 2359296 | tf_op args[0]
  3.7 87.5 %shard_map.91 = bf16[24,2048]{1,0:T(8,128)(2,1)} custom-call(bf16[1,1024,576]{2,1,0:T(8,128)(2,1)} %copy.10.latent, bf16[24,2048]{1,0:T(8,128)(2,1)} %nope_h.1, bf16[24,1024]{1,0:T(8,128)(2,1)} %rope_h.1, bf16[24,576]{1,0:T(8,128)(2,1)} %new_h.1, bf16[16,128,512]{2,1,0:T(8,128)(2,1)} %ku_h.1, bf16[16,512,128]{2,1,0:T(8,128)(2,1)} %vu_h.1, s32[16]{0:T(128)} %owner.1, ...), custom_call_target="tpu_custom_call" | custom-call | flops 17179869184 | bytes 8388608 | tf_op jit(solution)/shard_map/pallas_call | solution.py:402
  91.2 1.5 %copy.13 = bf16[24,2048]{1,0:T(8,128)(2,1)} copy(bf16[24,2048]{1,0:T(8,128)(2,1)} %shard_map.91) | data formatting | bytes 196608

commit v2 on v1

--- a/solution.py
+++ b/solution.py
@@ -16,8 +16,9 @@
 ROWS = PL * HL
 LAT, ROPE, NOPE, DV = 512, 64, 128, 128
 QW = LAT + 2 * ROPE
-SHARD, CH = 1024, 512
-PK = CH + CH * ROPE // LAT
+SHARD, SUB = 1024, 256
+CH = 2 * SUB
+KW = LAT + ROPE
 RB = 256
 
 
@@ -39,7 +40,7 @@
 
 def kernel(
     latent, nope_h, rope_h, new_h, ku_h, vu_h, owner, length, labels, out,
-    nope, rope, new, ku, vu, rtmp, kv, stage, qsend, q, qhi, mtop, tot, acc, osend, orecv,
+    nope, rope, new, ku, vu, kv, stage, qsend, q, mtop, tot, acc, osend, orecv,
     lsem, qss, qrs, kss, krs, vss, vrs, oss, ors,
 ):
     r, t = lax.axis_index("rep"), lax.axis_index("tp")
@@ -55,19 +56,16 @@
     partner = dev(y, xh * 2 + 1 - xl, z, 1 - c)
     slot = (y * 2 + xh) * 2 + xl
 
-    base = jnp.where(role_a, 0, 16)
+    base = jnp.where(role_a, 0, 32)
     loads = [
         pltpu.make_async_copy(nope_h, nope, lsem.at[0]),
         pltpu.make_async_copy(rope_h, rope, lsem.at[1]),
         pltpu.make_async_copy(new_h, new, lsem.at[2]),
         pltpu.make_async_copy(ku_h, ku, lsem.at[3]),
-        pltpu.make_async_copy(latent.at[0, :, pl.ds(LAT, ROPE)], rtmp, lsem.at[4]),
-        pltpu.make_async_copy(latent.at[0, pl.ds(0, CH), pl.ds(0, LAT)], kv.at[base, pl.ds(0, CH)], lsem.at[5]),
-        pltpu.make_async_copy(latent.at[0, pl.ds(CH, CH), pl.ds(0, LAT)], kv.at[base + 1, pl.ds(0, CH)], lsem.at[6]),
-    ]
+    ] + [pltpu.make_async_copy(latent.at[0, :, pl.ds(u * SUB, SUB)], kv.at[base + u], lsem.at[4 + u]) for u in range(4)]
     for load in loads:
         load.start()
-    vload = pltpu.make_async_copy(vu_h, vu, lsem.at[7])
+    vload = pltpu.make_async_copy(vu_h, vu, lsem.at[8])
     pl.when(role_a)(vload.start)
 
     barrier = pltpu.get_barrier_semaphore()
@@ -87,20 +85,9 @@
     lax.fori_loop(0, 16, greet_core, 0)
     lax.fori_loop(0, 8, greet_col, 0)
 
-    for i in (4, 5, 6):
-        loads[i].wait()
-    spread = iota((ROPE, 2 * ROPE), 0) - iota((ROPE, 2 * ROPE), 1)
-    lo_e, hi_e = (spread == 0).astype(BF16), (spread == -ROPE).astype(BF16)
-    half = CH // 2
-    for k in range(2):
-        packed = dot(rtmp[pl.ds(k * CH, half), :], lo_e) + dot(rtmp[pl.ds(k * CH + half, half), :], hi_e)
-        packed = packed.astype(BF16)
-        for j in range(4):
-            kv[base + k, pl.ds(CH, PK - CH), pl.ds(128 * j, 128)] = packed[64 * j : 64 * j + 64]
-
-    lab = labels[...]
+    lab_row = labels[...]
     sub, lane = iota((S, S), 0), iota((S, S), 1)
-    lab_row = jnp.sum(jnp.where(sub == lane, lab.astype(F32), 0.0), axis=0, keepdims=True).astype(jnp.int32)
+    lab = jnp.sum(jnp.where(sub == lane, lab_row.astype(F32), 0.0), axis=1, keepdims=True).astype(jnp.int32)
     same = lab == lab_row
     rank_row = jnp.sum(jnp.where(same & (sub < lane), 1.0, 0.0), axis=0, keepdims=True).astype(jnp.int32)
     rank_col = jnp.sum(jnp.where(same & (lane < sub), 1.0, 0.0), axis=1, keepdims=True).astype(jnp.int32)
@@ -114,8 +101,8 @@
     place = (iota((PL, S), 0) == slot_row * CAP + rank_row).astype(BF16)
     unplace = (iota((S, PL), 1) == slot_col * CAP + rank_col).astype(BF16)
 
-    for i in (0, 1, 2, 3):
-        loads[i].wait()
+    for load in loads:
+        load.wait()
     scale = (NOPE + ROPE) ** -0.5
     nope_s = dot(place, nope[...]).astype(BF16)
     rope_s = dot(place, rope[...]) * scale
@@ -156,36 +143,48 @@
             src_ref=kv.at[src], dst_ref=kv.at[dst], send_sem=kss.at[sem], recv_sem=krs.at[dst], device_id=d, device_id_type=MESH
         )
 
-    o = jnp.where(role_a, 0, 8)
-
-    def ring_own(k):
-        return [kv_copy(o + k, o + 2 + k, k, zp), kv_copy(o + k, o + 4 + k, 2 + k, zm), kv_copy(o + k, o + k, 8 + k, sib)]
-
-    def ring_pass(k):
-        out_ = [kv_copy(o + k, o + k, 8 + k, sib)]
-        if k == 2:
-            out_.insert(0, kv_copy(o + 2, o + 6, 4, zp))
-        if k == 5:
-            out_.insert(0, kv_copy(o + 5, o + 7, 5, zm))
+    o = jnp.where(role_a, 0, 16)
+
+    def ring_own(u):
+        return [kv_copy(o + u, o + 4 + u, u, zp), kv_copy(o + u, o + 8 + u, 4 + u, zm), kv_copy(o + u, o + u, 12 + u, sib)]
+
+    def pair(j):
+        if j < 2:
+            return 2 * j, 2 * j + 1
+        return (2 + j, 8 + (j - 2 ^ 1)) if j < 6 else (2 * j, 2 * j + 1)
+
+    def ring_pass(j):
+        a, b = pair(j)
+        out_ = [kv_copy(o + k, o + k, 12 + k, sib) for k in (a, b)]
+        if j in (2, 4):
+            out_ = [kv_copy(o + a, o + 10 + j, 6 + j, zp), kv_copy(o + b, o + 11 + j, 7 + j, zm)] + out_
         return out_
 
     def arrived(k):
         kv_copy(k, k, 0, sib).wait_recv()
 
-    def ring_step(k):
-        arrived(o + k)
-        for cp in ring_pass(k):
+    def ring_step(j):
+        for k in pair(j):
+            arrived(o + k)
+        for cp in ring_pass(j):
             cp.start()
 
-    cross = [kv_copy(16 + k, 8 + k, 16 + k, partner) for k in range(2)]
+    def cross_step(u):
+        arrived(16 + u)
+        for cp in ring_own(u):
+            cp.start()
+
+    cross = [kv_copy(32 + u, 16 + u, 28 + u, partner) for u in range(4)]
 
     pl.semaphore_wait(barrier, jnp.where(role_a, 25, 26))
 
     @pl.when(role_a)
     def _():
-        for k in range(2):
-            for cp in ring_own(k):
-                cp.start()
+        by_part = [ring_own(u) for u in range(4)]
+        for u in range(4):
+            by_part[u][0].start()
+            by_part[u ^ 1][1].start()
+            by_part[u][2].start()
 
     def q_send(i, _):
         s = (slot + i) % SLOTS
@@ -208,14 +207,8 @@
 
     @pl.when(role_a)
     def _():
-        for k in (2, 4, 3, 5):
-            ring_step(k)
-
-    @pl.when(jnp.logical_not(role_a))
-    def _():
-        arrived(8)
-        for cp in ring_own(0):
-            cp.start()
+        for j in (2, 3, 4):
+            ring_step(j)
 
     def q_wait(i, _):
         g = (r + i) % SLOTS
@@ -241,17 +234,11 @@
         for k in range(2)
     ]
 
-    @pl.when(role_a)
-    def _():
-        for cp in halves:
-            cp.start()
-
     q3 = q[...]
     tail = q3[:, LAT:].astype(F32)
     wide_low = iota((ROWS, 2 * ROPE), 1) < ROPE
     stage[0] = tail
     tail = jnp.where(wide_low, tail, 0.0)
-    qhi[...] = pltpu.roll(tail, ROPE, 1).astype(BF16)
     pieces = [stage[0, pl.ds(k, PL, stride=HL), :] for k in range(9)]
     new_p = []
     for k in range(5):
@@ -265,57 +252,72 @@
     for j in range(4):
         acc[j] = own_keys[:, 128 * j : 128 * j + 128]
     mtop[...] = jnp.broadcast_to(own_score, mtop.shape)
-    tot[...] = jnp.ones_like(tot)
-    q[:, pl.ds(LAT, 2 * ROPE)] = tail.astype(BF16)
-
-    def attend(ci):
-        place_z = (ci % 8) // 2
-        zz = (z + jnp.where(place_z == 1, 3, jnp.where(place_z == 2, 1, jnp.where(place_z == 3, 2, 0)))) % 4
-        first = (zz * 2 + jnp.where(ci < 8, xl, 1 - xl)) * SHARD + (ci % 2) * CH
-        keys = kv[ci, pl.ds(0, CH), :]
-        rot = kv[ci, pl.ds(CH, PK - CH), :]
-        rot = jnp.concatenate([rot[:, 128 * j : 128 * j + 128] for j in range(4)], axis=0)
-        k_lo = jnp.concatenate([keys[:half], rot], axis=1)
-        k_hi = jnp.concatenate([keys[half:], rot], axis=1)
-        bias = jnp.where(first + iota((1, CH), 1) < live, 0.0, NEG)
+    tot[...] = (iota((ROWS, 128), 1) == 0).astype(F32)
+
+    def attend(ka, kb):
+        def first(k):
+            s = k % 16 // 4
+            zz = (z + jnp.where(s == 1, 3, jnp.where(s == 2, 1, jnp.where(s == 3, 2, 0)))) % 4
+            return (zz * 2 + jnp.where(k < 16, xl, 1 - xl)) * SHARD + k % 4 * SUB
+
+        keys = jnp.concatenate([kv[ka], kv[kb]], axis=1)
+        lane = iota((1, CH), 1)
+        at = lane + jnp.where(lane < SUB, first(ka), first(kb) - SUB)
+        bias = jnp.where(at < live, 0.0, NEG)
+
+        def score(b):
+            return dot(q[pl.ds(b * RB, RB), pl.ds(0, KW)], keys) + bias
+
+        following = score(0)
         for b in range(ROWS // RB):
-            rs = pl.ds(b * RB, RB)
-            s_lo = dot_nt(q[rs, :], k_lo)
-            s_hi = dot_nt(jnp.concatenate([q[rs, pl.ds(0, LAT)], qhi[rs, :]], axis=1), k_hi)
-            s = jnp.concatenate([s_lo, s_hi], axis=1) + bias
-            top = mtop[rs, pl.ds(0, 1)]
-            new_top = jnp.maximum(top, jnp.max(s, axis=1, keepdims=True))
+            rs, s = pl.ds(b * RB, RB), following
+            if (b + 1) * RB < ROWS:
+                following = score(b + 1)
+            tiles = [s[:, 128 * j : 128 * j + 128] for j in range(CH // 128)]
+            top = mtop[rs, :]
+            new_top = jnp.maximum(top, jnp.max(functools.reduce(jnp.maximum, tiles), axis=1, keepdims=True))
             shrink = jnp.exp(top - new_top)
-            w = jnp.exp(s - new_top)
-            tot[rs, :] = jnp.broadcast_to(tot[rs, pl.ds(0, 1)] * shrink + jnp.sum(w, axis=1, keepdims=True), (RB, 128))
-            mtop[rs, :] = jnp.broadcast_to(new_top, (RB, 128))
-            new = dot(w.astype(BF16), keys)
+            weights = [jnp.exp(a - new_top) for a in tiles]
+            tot[rs, :] = tot[rs, :] * shrink + functools.reduce(jnp.add, weights)
+            mtop[rs, :] = new_top
+            new = dot_nt(jnp.concatenate([a.astype(BF16) for a in weights], axis=1), keys[:LAT])
             for j in range(4):
                 acc[j, rs, :] = acc[j, rs, :] * shrink + new[:, 128 * j : 128 * j + 128]
 
     def step(i, _):
-        ci = i + (i % 8 == 3).astype(jnp.int32) - (i % 8 == 4).astype(jnp.int32)
+        j = i % 8
+        inner = jnp.logical_and(j >= 2, j < 6)
+        ka = jnp.where(inner, 2 + j, 2 * j) + i // 8 * 16
+        kb = jnp.where(inner, 7 + j - j % 2 * 2, 2 * j + 1) + i // 8 * 16
 
         @pl.when(role_a)
         def _():
-            for at, k in ((5, 6), (6, 7)):
+            for at, k in ((1, 5), (3, 6), (5, 7)):
                 pl.when(i == at)(functools.partial(ring_step, k))
-            pl.when(i >= 8)(lambda: arrived(ci))
+
+            @pl.when(i == 6)
+            def _():
+                for cp in halves:
+                    cp.start()
+
+            @pl.when(i >= 8)
+            def _():
+                arrived(ka)
+                arrived(kb)
 
         @pl.when(jnp.logical_not(role_a))
         def _():
-            pl.when(i < 8)(lambda: arrived(ci))
-
-            @pl.when(i == 2)
+            @pl.when(i < 8)
             def _():
-                arrived(9)
-                for cp in ring_own(1):
-                    cp.start()
-
-            for at, k in ((9, 2), (10, 4), (11, 3), (12, 5), (13, 6), (14, 7)):
+                arrived(ka)
+                arrived(kb)
+
+            for u in range(4):
+                pl.when(i == 2 + 2 * u)(functools.partial(cross_step, u))
+            for at, k in ((9, 2), (10, 3), (12, 4), (13, 5), (14, 6), (15, 7)):
                 pl.when(i == at)(functools.partial(ring_step, k))
 
-        attend(ci)
+        attend(ka, kb)
         return 0
 
     lax.fori_loop(0, 16, step, 0)
@@ -331,7 +333,7 @@
 
     for h in range(HL):
         rows = pl.ds(h, PL, stride=HL)
-        total = tot[rows, :]
+        total = jnp.sum(tot[rows, :], axis=1, keepdims=True)
         mean = jnp.concatenate([acc[j, rows, :] / total for j in range(4)], axis=1).astype(BF16)
         stage[0, rows, :] = dot(mean, vu[h])
     osend[...] = stage[0].astype(BF16)
@@ -363,11 +365,11 @@
         for cp in cross:
             cp.wait_send()
 
-    for k in range(2):
-        for cp in ring_own(k):
+    for u in range(4):
+        for cp in ring_own(u):
             cp.wait_send()
-    for k in range(2, 8):
-        for cp in ring_pass(k):
+    for j in range(2, 8):
+        for cp in ring_pass(j):
             cp.wait_send()
 
     def all_wait(i, _):
@@ -410,23 +412,24 @@
             pltpu.VMEM(new_latent.shape, BF16),
             pltpu.VMEM(key_up.shape, BF16),
             pltpu.VMEM(value_up.shape, BF16),
-            pltpu.VMEM((SHARD, ROPE), BF16),
-            pltpu.VMEM((18, PK, LAT), BF16),
+            pltpu.VMEM((36, KW, SUB), BF16),
             pltpu.VMEM((5, ROWS, 128), F32),
             pltpu.VMEM((ROWS, QW), BF16),
             pltpu.VMEM((ROWS, QW), BF16),
-            pltpu.VMEM((ROWS, 2 * ROPE), BF16),
             pltpu.VMEM((ROWS, 128), F32),
             pltpu.VMEM((ROWS, 128), F32),
             pltpu.VMEM((4, ROWS, 128), F32),
             pltpu.VMEM((ROWS, DV), BF16),
             pltpu.VMEM((ROWS, DV), BF16),
-            dma((8,)), dma((SLOTS,)), dma((SLOTS,)), dma((18,)), dma((16,)),
+            dma((9,)), dma((SLOTS,)), dma((SLOTS,)), dma((32,)), dma((32,)),
             dma((2,)), dma((2,)), dma((SLOTS,)), dma((SLOTS,)),
         ],
         compiler_params=pltpu.CompilerParams(collective_id=0, has_side_effects=True, vmem_limit_bytes=56 << 20),
         cost_estimate=pl.CostEstimate(flops=16 << 30, bytes_accessed=8 << 20, transcendentals=8 << 20),
-    )(latent_cache, query_nope, query_rope, new_latent, key_up, value_up, prompt_owner, prompt_length, sample_prompt)
+    )(
+        jnp.swapaxes(latent_cache, 1, 2), query_nope, query_rope, new_latent, key_up, value_up,
+        prompt_owner, prompt_length, sample_prompt.reshape(1, -1),
+    )
 
 
 def solution(mesh):

time: 93.3 us -> 63.9 us (0.68)
  Pallas kernels: 87.5 us -> 62.2 us
  local copies, waits for them, and re-layouts: 5.29 us -> 1.54 us
    pallas_call x1, Pallas kernels: 87.5 us -> 62.2 us  [shards(): pl.pallas_call(kernel, out_shape=jax.ShapeDtypeStruct(query_nope.shape, B...]
    unnamed x3 -> x1, local copies, waits for them, and re-layouts: 5.29 us -> 1.54 us
where the time goes in v2:
time: 63.9 us; the launch traced here: 63.7 us
  Pallas kernels  62.2 us (97%)
  local copies, waits for them, and re-layouts  1.54 us (2%)
    pallas_call x1, Pallas kernels, shards(): pl.pallas_call(kernel, out_shape=jax.ShapeDtypeStruct(query_nope.shape, B...  62.2 us
    unnamed x1, local copies, waits for them, and re-layouts  1.54 us

profile of v2, /device:TPU:1, one launch (start us, length us, event | category | flops | bytes accessed | tf_op | source)
XLA Modules:
  0.0 63.7 jit_solution(8795147240714975497)
XLA Ops:
  0.0 62.2 %shard_map.91 = bf16[24,2048]{1,0:T(8,128)(2,1)} custom-call(bf16[1,576,1024]{2,1,0:T(8,128)(2,1)} %bitcast.2, bf16[24,2048]{1,0:T(8,128)(2,1)} %nope_h.1, bf16[24,1024]{1,0:T(8,128)(2,1)} %rope_h.1, bf16[24,576]{1,0:T(8,128)(2,1)} %new_h.1, bf16[16,128,512]{2,1,0:T(8,128)(2,1)} %ku_h.1, bf16[16,512,128]{2,1,0:T(8,128)(2,1)} %vu_h.1, s32[16]{0:T(128)} %owner.1, ...), custom_call_target="tpu_custom_call" | custom-call | flops 17179869184 | bytes 8388608 | tf_op jit(solution)/shard_map/pallas_call | solution.py:404
  62.2 1.5 %copy.11 = bf16[24,2048]{1,0:T(8,128)(2,1)} copy(bf16[24,2048]{1,0:T(8,128)(2,1)} %shard_map.91) | data formatting | bytes 196608

commit v3 on v2

--- a/solution.py
+++ b/solution.py
@@ -19,7 +19,9 @@
 SHARD, SUB = 1024, 256
 CH = 2 * SUB
 KW = LAT + ROPE
-RB = 256
+RB = SLOTS * HL
+NEAR_HEADS = 6
+EARLY = 5
 
 
 def dot(a, b):
@@ -30,8 +32,12 @@
     return lax.dot_general(a, b, (((1,), (1,)), ((), ())), preferred_element_type=F32)
 
 
+def swap(n, i):
+    return sum((n // b % 2 + i // b % 2 - 2 * (n // b % 2) * (i // b % 2)) * b for b in (1, 2, 4, 8))
+
+
 def block(i):
-    return pl.ds(pl.multiple_of(i * (CAP * HL), 16), CAP * HL)
+    return pl.ds(pl.multiple_of(i * HL, HL), HL)
 
 
 def iota(shape, dim):
@@ -40,7 +46,7 @@
 
 def kernel(
     latent, nope_h, rope_h, new_h, ku_h, vu_h, owner, length, labels, out,
-    nope, rope, new, ku, vu, kv, stage, qsend, q, mtop, tot, acc, osend, orecv,
+    nope, rope, new, ku, vu, kv, stage, qsend, q, mtop, tot, acc, osend, orecv, unplace,
     lsem, qss, qrs, kss, krs, vss, vrs, oss, ors,
 ):
     r, t = lax.axis_index("rep"), lax.axis_index("tp")
@@ -98,8 +104,8 @@
         slot_row = jnp.where(lab_row == p, own, slot_row)
         slot_col = jnp.where(lab == p, own, slot_col)
         live = live + jnp.where(own == slot, length[p], 0)
-    place = (iota((PL, S), 0) == slot_row * CAP + rank_row).astype(BF16)
-    unplace = (iota((S, PL), 1) == slot_col * CAP + rank_col).astype(BF16)
+    place = (iota((PL, S), 0) == rank_row * SLOTS + slot_row).astype(BF16)
+    code = rank_col * SLOTS + slot_col
 
     for load in loads:
         load.wait()
@@ -109,7 +115,7 @@
     new_s = dot(place, new[...])
     new_s = jnp.concatenate([new_s[:, :LAT], jnp.concatenate([new_s[:, LAT:], jnp.zeros((PL, ROPE), F32)], axis=1)], axis=1)
     low = iota((PL, 2 * ROPE), 1) < ROPE
-    for h in range(HL):
+    def absorb(h):
         rows = pl.ds(h, PL, stride=HL)
         lat_q = dot(nope_s[:, NOPE * h : NOPE * (h + 1)], ku[h]) * scale
         for j in range(4):
@@ -125,18 +131,22 @@
         else:
             piece = jnp.zeros_like(mine)
         stage[4, rows, :] = jnp.where(low, mine, piece)
-    for j in range(5):
-        qsend[:, pl.ds(128 * j, 128)] = stage[j].astype(BF16)
-
-    def q_copy(s, d):
+    for h in range(HL // 2):
+        absorb(h)
+
+    places = (pl.ds(0, 1), pl.ds(1, 2))
+
+    def q_copy(n, s, d):
         return pltpu.make_async_remote_copy(
-            src_ref=qsend.at[block(s)], dst_ref=q.at[block(r)], send_sem=qss.at[s], recv_sem=qrs.at[r], device_id=d, device_id_type=MESH
+            src_ref=qsend.at[places[n], block(s)], dst_ref=q.at[places[n], block(r)],
+            send_sem=qss.at[n * SLOTS + s], recv_sem=qrs.at[n * SLOTS + r], device_id=d, device_id_type=MESH,
         )
 
     def q_dev(s):
         return dev(s // 4, ((s // 2) % 2) * 2 + s % 2, z, xl)
 
-    own_q = pltpu.make_async_copy(qsend.at[block(r)], q.at[block(r)], qrs.at[r])
+    def own_q(n):
+        return pltpu.make_async_copy(qsend.at[places[n], block(r)], q.at[places[n], block(r)], qrs.at[n * SLOTS + r])
 
     def kv_copy(src, dst, sem, d):
         return pltpu.make_async_remote_copy(
@@ -186,75 +196,73 @@
             by_part[u ^ 1][1].start()
             by_part[u][2].start()
 
-    def q_send(i, _):
-        s = (slot + i) % SLOTS
-
-        @pl.when(jnp.logical_and(role_a, i == 0))
-        def _():
-            own_q.start()
-
-        @pl.when(jnp.logical_not(jnp.logical_and(role_a, i == 0)))
-        def _():
-            q_copy(s, q_dev(s)).start()
-        return 0
-
-    lax.fori_loop(0, SLOTS, q_send, 0)
+    for h in range(HL // 2, HL):
+        absorb(h)
+    for j in range(5):
+        qsend[:, :, pl.ds(128 * j, 128)] = stage[j].astype(BF16).reshape(CAP, RB, 128)
+
+    def q_send(n, i, _):
+        s = swap(slot, i)
+        kept = jnp.logical_and(role_a, i == 0)
+        pl.when(kept)(lambda: own_q(n).start())
+        pl.when(jnp.logical_not(kept))(lambda: q_copy(n, s, q_dev(s)).start())
+        return 0
+
+    for n in range(2):
+        lax.fori_loop(0, SLOTS, functools.partial(q_send, n), 0)
 
     @pl.when(jnp.logical_not(role_a))
     def _():
         for cp in cross:
             cp.start()
 
-    @pl.when(role_a)
-    def _():
-        for j in (2, 3, 4):
-            ring_step(j)
-
-    def q_wait(i, _):
+    def q_wait(n, i, _):
         g = (r + i) % SLOTS
-
-        @pl.when(jnp.logical_and(role_a, i == 0))
-        def _():
-            own_q.wait()
-
-        @pl.when(jnp.logical_not(jnp.logical_and(role_a, i == 0)))
+        kept = jnp.logical_and(role_a, i == 0)
+        pl.when(kept)(lambda: own_q(n).wait())
+
+        @pl.when(jnp.logical_not(kept))
         def _():
             pltpu.make_async_remote_copy(
-                src_ref=qsend.at[block(0)], dst_ref=q.at[block(g)], send_sem=qss.at[0], recv_sem=qrs.at[g], device_id=sib, device_id_type=MESH
+                src_ref=qsend.at[places[n], block(0)], dst_ref=q.at[places[n], block(g)],
+                send_sem=qss.at[0], recv_sem=qrs.at[n * SLOTS + g], device_id=sib, device_id_type=MESH,
             ).wait_recv()
         return 0
 
-    lax.fori_loop(0, SLOTS, q_wait, 0)
-
-    halves = [
-        pltpu.make_async_remote_copy(
-            src_ref=vu_h.at[pl.ds(8 * k, 8)], dst_ref=vu.at[pl.ds(8 * k, 8)], send_sem=vss.at[k], recv_sem=vrs.at[k],
+    def value_part(k, first, count):
+        return pltpu.make_async_remote_copy(
+            src_ref=vu_h.at[pl.ds(first, count)], dst_ref=vu.at[pl.ds(first, count)], send_sem=vss.at[k], recv_sem=vrs.at[k],
             device_id=dev(y, (xh if k == 0 else 1 - xh) * 2 + 1 - xl, z, c), device_id_type=MESH,
         )
-        for k in range(2)
-    ]
-
-    q3 = q[...]
-    tail = q3[:, LAT:].astype(F32)
-    wide_low = iota((ROWS, 2 * ROPE), 1) < ROPE
-    stage[0] = tail
-    tail = jnp.where(wide_low, tail, 0.0)
-    pieces = [stage[0, pl.ds(k, PL, stride=HL), :] for k in range(9)]
-    new_p = []
-    for k in range(5):
-        left = pltpu.roll(pieces[2 * k], ROPE, 1)
-        new_p.append(jnp.where(low, left, pieces[2 * k + 1] if k < 4 else 0.0))
-    new_p = jnp.concatenate(new_p, axis=1).astype(BF16)
-    by_row = (iota((ROWS, PL), 0) // HL == iota((ROWS, PL), 1)).astype(BF16)
-    own_keys = dot(by_row, new_p)
-    own_score = jnp.sum(q3[:, :LAT].astype(F32) * own_keys[:, :LAT], axis=1, keepdims=True)
-    own_score = own_score + jnp.sum(tail * own_keys[:, LAT:], axis=1, keepdims=True)
-    for j in range(4):
-        acc[j] = own_keys[:, 128 * j : 128 * j + 128]
-    mtop[...] = jnp.broadcast_to(own_score, mtop.shape)
-    tot[...] = (iota((ROWS, 128), 1) == 0).astype(F32)
-
-    def attend(ka, kb):
+
+    halves = [value_part(0, 0, NEAR_HEADS), value_part(1, NEAR_HEADS, HL - NEAR_HEADS)]
+
+    wanted = jnp.concatenate([code * HL + h for h in range(HL)], axis=0)
+    unplace[...] = (iota((HL * S, ROWS), 1) == wanted).astype(BF16)
+
+    low_b = low[:SLOTS]
+    wide_low = iota((RB, 2 * ROPE), 1) < ROPE
+    by_row = (iota((RB, SLOTS), 0) // HL == iota((RB, SLOTS), 1)).astype(BF16)
+
+    def open_block(b):
+        rs = pl.ds(b * RB, RB)
+        qb = q[b]
+        tail = qb[:, LAT:].astype(F32)
+        stage[0, rs, :] = tail
+        pieces = [stage[0, pl.ds(b * RB + k, SLOTS, stride=HL), :] for k in range(9)]
+        new_p = []
+        for k in range(5):
+            left = pltpu.roll(pieces[2 * k], ROPE, 1)
+            new_p.append(jnp.where(low_b, left, pieces[2 * k + 1] if k < 4 else 0.0))
+        own_keys = dot(by_row, jnp.concatenate(new_p, axis=1).astype(BF16))
+        own_score = jnp.sum(qb[:, :LAT].astype(F32) * own_keys[:, :LAT], axis=1, keepdims=True)
+        own_score = own_score + jnp.sum(jnp.where(wide_low, tail, 0.0) * own_keys[:, LAT:], axis=1, keepdims=True)
+        for j in range(4):
+            acc[j, rs, :] = own_keys[:, 128 * j : 128 * j + 128]
+        mtop[rs, :] = jnp.broadcast_to(own_score, (RB, 128))
+        tot[rs, :] = (iota((RB, 128), 1) == 0).astype(F32)
+
+    def attend(ka, kb, blocks):
         def first(k):
             s = k % 16 // 4
             zz = (z + jnp.where(s == 1, 3, jnp.where(s == 2, 1, jnp.where(s == 3, 2, 0)))) % 4
@@ -266,12 +274,12 @@
         bias = jnp.where(at < live, 0.0, NEG)
 
         def score(b):
-            return dot(q[pl.ds(b * RB, RB), pl.ds(0, KW)], keys) + bias
-
-        following = score(0)
-        for b in range(ROWS // RB):
+            return dot(q[b, :, pl.ds(0, KW)], keys) + bias
+
+        following = score(blocks[0])
+        for b in blocks:
             rs, s = pl.ds(b * RB, RB), following
-            if (b + 1) * RB < ROWS:
+            if b != blocks[-1]:
                 following = score(b + 1)
             tiles = [s[:, 128 * j : 128 * j + 128] for j in range(CH // 128)]
             top = mtop[rs, :]
@@ -284,43 +292,52 @@
             for j in range(4):
                 acc[j, rs, :] = acc[j, rs, :] * shrink + new[:, 128 * j : 128 * j + 128]
 
-    def step(i, _):
+    turns_a = {0: {2: 2, 3: 3, 4: 4}, 1: {1: 5, 4: 6}, 2: {7: 7}}
+    turns_x = {0: {}, 1: {2: 0, 4: 1}, 2: {7: 2, 8: 3}}
+    turns_b = {0: {}, 1: {}, 2: {9: 2, 10: 3, 12: 4, 13: 5, 14: 6, 15: 7}}
+
+    def step(loop, blocks, i, _):
         j = i % 8
         inner = jnp.logical_and(j >= 2, j < 6)
         ka = jnp.where(inner, 2 + j, 2 * j) + i // 8 * 16
         kb = jnp.where(inner, 7 + j - j % 2 * 2, 2 * j + 1) + i // 8 * 16
 
+        def both():
+            arrived(ka)
+            arrived(kb)
+
         @pl.when(role_a)
         def _():
-            for at, k in ((1, 5), (3, 6), (5, 7)):
+            for at, k in turns_a[loop].items():
                 pl.when(i == at)(functools.partial(ring_step, k))
-
-            @pl.when(i == 6)
-            def _():
-                for cp in halves:
-                    cp.start()
-
-            @pl.when(i >= 8)
-            def _():
-                arrived(ka)
-                arrived(kb)
+            if loop == 2:
+
+                pl.when(i == 5)(halves[1].start)
+                pl.when(i == 8)(halves[0].start)
+                pl.when(i >= 8)(both)
 
         @pl.when(jnp.logical_not(role_a))
         def _():
-            @pl.when(i < 8)
-            def _():
-                arrived(ka)
-                arrived(kb)
-
-            for u in range(4):
-                pl.when(i == 2 + 2 * u)(functools.partial(cross_step, u))
-            for at, k in ((9, 2), (10, 3), (12, 4), (13, 5), (14, 6), (15, 7)):
+            for at, k in turns_x[loop].items():
+                pl.when(i == at)(functools.partial(cross_step, k))
+            for at, k in turns_b[loop].items():
                 pl.when(i == at)(functools.partial(ring_step, k))
-
-        attend(ka, kb)
-        return 0
-
-    lax.fori_loop(0, 16, step, 0)
+            if loop == 0:
+                both()
+            if loop == 2:
+                pl.when(i < 8)(both)
+
+        attend(ka, kb, blocks)
+        return 0
+
+    lax.fori_loop(0, SLOTS, functools.partial(q_wait, 0), 0)
+    open_block(0)
+    lax.fori_loop(0, EARLY, functools.partial(step, 0, (0,)), 0)
+    lax.fori_loop(0, SLOTS, functools.partial(q_wait, 1), 0)
+    open_block(1)
+    open_block(2)
+    lax.fori_loop(0, EARLY, functools.partial(step, 1, (1, 2)), 0)
+    lax.fori_loop(EARLY, 16, functools.partial(step, 2, (0, 1, 2)), 0)
 
     @pl.when(role_a)
     def _():
@@ -333,18 +350,18 @@
 
     for h in range(HL):
         rows = pl.ds(h, PL, stride=HL)
-        total = jnp.sum(tot[rows, :], axis=1, keepdims=True)
-        mean = jnp.concatenate([acc[j, rows, :] / total for j in range(4)], axis=1).astype(BF16)
+        share = 1.0 / jnp.sum(tot[rows, :], axis=1, keepdims=True)
+        mean = jnp.concatenate([acc[j, rows, :] * share for j in range(4)], axis=1).astype(BF16)
         stage[0, rows, :] = dot(mean, vu[h])
-    osend[...] = stage[0].astype(BF16)
+    osend[...] = stage[0].astype(BF16).reshape(CAP, RB, DV)
 
     def o_copy(g):
         return pltpu.make_async_remote_copy(
-            src_ref=osend.at[block(g)], dst_ref=orecv.at[block(slot)], send_sem=oss.at[g], recv_sem=ors.at[slot],
+            src_ref=osend.at[:, block(g)], dst_ref=orecv.at[:, block(slot)], send_sem=oss.at[g], recv_sem=ors.at[slot],
             device_id=(g, z * 2 + c), device_id_type=MESH,
         )
 
-    own_o = pltpu.make_async_copy(osend.at[block(r)], orecv.at[block(r)], ors.at[r])
+    own_o = pltpu.make_async_copy(osend.at[:, block(r)], orecv.at[:, block(r)], ors.at[r])
 
     def o_send(i, _):
         g = (r + i) % SLOTS
@@ -383,19 +400,19 @@
 
         @pl.when(jnp.logical_not(kept))
         def _():
-            q_copy(s, sib).wait_send()
+            q_copy(0, s, sib).wait_send()
+            q_copy(1, s, sib).wait_send()
             o_copy(g).wait_send()
             pltpu.make_async_remote_copy(
-                src_ref=osend.at[block(0)], dst_ref=orecv.at[block(s)], send_sem=oss.at[0], recv_sem=ors.at[s],
+                src_ref=osend.at[:, block(0)], dst_ref=orecv.at[:, block(s)], send_sem=oss.at[0], recv_sem=ors.at[s],
                 device_id=sib, device_id_type=MESH,
             ).wait_recv()
         return 0
 
     lax.fori_loop(0, SLOTS, all_wait, 0)
-    stage[0] = orecv[...].astype(F32)
+    picked = dot(unplace[...], orecv[...].reshape(ROWS, DV))
     for h in range(HL):
-        picked = stage[0, pl.ds(h, PL, stride=HL), :].astype(BF16)
-        out[:, pl.ds(DV * h, DV)] = dot(unplace, picked).astype(BF16)
+        out[:, pl.ds(DV * h, DV)] = picked[S * h : S * (h + 1)].astype(BF16)
 
 
 def shards(latent_cache, query_nope, query_rope, new_latent, key_up, value_up, prompt_owner, prompt_length, sample_prompt):
@@ -403,7 +420,7 @@
     dma = pltpu.SemaphoreType.DMA
     return pl.pallas_call(
         kernel,
-        out_shape=jax.ShapeDtypeStruct(query_nope.shape, BF16),
+        out_shape=pltpu.VMEM(query_nope.shape, BF16),
         in_specs=[hbm] * 6 + [smem] * 2 + [vmem],
         out_specs=vmem,
         scratch_shapes=[
@@ -414,14 +431,15 @@
             pltpu.VMEM(value_up.shape, BF16),
             pltpu.VMEM((36, KW, SUB), BF16),
             pltpu.VMEM((5, ROWS, 128), F32),
-            pltpu.VMEM((ROWS, QW), BF16),
-            pltpu.VMEM((ROWS, QW), BF16),
+            pltpu.VMEM((CAP, RB, QW), BF16),
+            pltpu.VMEM((CAP, RB, QW), BF16),
             pltpu.VMEM((ROWS, 128), F32),
             pltpu.VMEM((ROWS, 128), F32),
             pltpu.VMEM((4, ROWS, 128), F32),
-            pltpu.VMEM((ROWS, DV), BF16),
-            pltpu.VMEM((ROWS, DV), BF16),
-            dma((9,)), dma((SLOTS,)), dma((SLOTS,)), dma((32,)), dma((32,)),
+            pltpu.VMEM((CAP, RB, DV), BF16),
+            pltpu.VMEM((CAP, RB, DV), BF16),
+            pltpu.VMEM((HL * S, ROWS), BF16),
+            dma((9,)), dma((2 * SLOTS,)), dma((2 * SLOTS,)), dma((32,)), dma((32,)),
             dma((2,)), dma((2,)), dma((SLOTS,)), dma((SLOTS,)),
         ],
         compiler_params=pltpu.CompilerParams(collective_id=0, has_side_effects=True, vmem_limit_bytes=56 << 20),

time: 63.9 us -> 62 us (0.970)
  Pallas kernels: 62.2 us -> 61.2 us
  local copies, waits for them, and re-layouts: 1.54 us -> 0.64 us
    pallas_call x1, Pallas kernels: 62.2 us -> 61.2 us  [shards(): pl.pallas_call(kernel, out_shape=pltpu.VMEM(query_nope.shape, BF16), in_s...]
    unnamed x1, local copies, waits for them, and re-layouts: 1.54 us -> 0.64 us
where the time goes in v3:
time: 62 us; the launch traced here: 61.9 us
  Pallas kernels  61.2 us (99%)
  local copies, waits for them, and re-layouts  0.64 us (1%)
    pallas_call x1, Pallas kernels, shards(): pl.pallas_call(kernel, out_shape=pltpu.VMEM(query_nope.shape, BF16), in_s...  61.2 us

profile of v3, /device:TPU:1, one launch (start us, length us, event | category | flops | bytes accessed | tf_op | source)
XLA Modules:
  0.0 61.9 jit_solution(899025521668834508)
XLA Ops:
  0.0 61.2 %shard_map.91 = bf16[24,2048]{1,0:T(8,128)(2,1)S(1)} custom-call(bf16[1,576,1024]{2,1,0:T(8,128)(2,1)} %bitcast.2, bf16[24,2048]{1,0:T(8,128)(2,1)} %nope_h.1, bf16[24,1024]{1,0:T(8,128)(2,1)} %rope_h.1, bf16[24,576]{1,0:T(8,128)(2,1)} %new_h.1, bf16[16,128,512]{2,1,0:T(8,128)(2,1)} %ku_h.1, bf16[16,512,128]{2,1,0:T(8,128)(2,1)} %vu_h.1, s32[16]{0:T(128)} %owner.1, ...), custom_call_target="tpu_custom_call" | custom-call | flops 17179869184 | bytes 8388608 | tf_op jit(solution)/shard_map/pallas_call | solution.py:421
  61.2 0.6 %copy.11 = bf16[24,2048]{1,0:T(8,128)(2,1)} copy(bf16[24,2048]{1,0:T(8,128)(2,1)S(1)} %shard_map.91) | data formatting | bytes 196608

commit v4 on v3

--- a/solution.py
+++ b/solution.py
@@ -17,7 +17,6 @@
 LAT, ROPE, NOPE, DV = 512, 64, 128, 128
 QW = LAT + 2 * ROPE
 SHARD, SUB = 1024, 256
-CH = 2 * SUB
 KW = LAT + ROPE
 RB = SLOTS * HL
 NEAR_HEADS = 6
@@ -45,8 +44,8 @@
 
 
 def kernel(
-    latent, nope_h, rope_h, new_h, ku_h, vu_h, owner, length, labels, out,
-    nope, rope, new, ku, vu, kv, stage, qsend, q, mtop, tot, acc, osend, orecv, unplace,
+    latent, nope_h, rope_h, new_h, ku_h, vu_h, owner_h, length_h, labels_h, out,
+    labels, owner, length, nope, rope, new, ku, vu, kv, stage, qsend, q, mtop, tot, acc, osend, orecv, unplace,
     lsem, qss, qrs, kss, krs, vss, vrs, oss, ors,
 ):
     r, t = lax.axis_index("rep"), lax.axis_index("tp")
@@ -61,6 +60,23 @@
     sib = dev(y, x, z, 1 - c)
     partner = dev(y, xh * 2 + 1 - xl, z, 1 - c)
     slot = (y * 2 + xh) * 2 + xl
+
+    barrier = pltpu.get_barrier_semaphore()
+
+    def greet(d):
+        pl.semaphore_signal(barrier, inc=1, device_id=d, device_id_type=MESH)
+
+    hops = (0, 1, 2, 1)
+    for i in sorted(range(16), key=lambda i: -hops[i // 4] - hops[i % 4]):
+        yy, xx = (y + i // 4) % 4, (x + i % 4) % 4
+        if i == 0:
+            pl.when(jnp.logical_not(role_a))(functools.partial(greet, dev(y, x, z, xl)))
+        else:
+            greet(dev(yy, xx, z, xl))
+        if i % 2 == 0:
+            greet(dev(yy, (xx + xl + c) % 4, z, 1 - xl))
+    for d in (zp, zm):
+        greet(d)
 
     base = jnp.where(role_a, 0, 32)
     loads = [
@@ -68,29 +84,17 @@
         pltpu.make_async_copy(rope_h, rope, lsem.at[1]),
         pltpu.make_async_copy(new_h, new, lsem.at[2]),
         pltpu.make_async_copy(ku_h, ku, lsem.at[3]),
+        pltpu.make_async_copy(labels_h, labels, lsem.at[9]),
+        pltpu.make_async_copy(owner_h, owner, lsem.at[10]),
+        pltpu.make_async_copy(length_h, length, lsem.at[11]),
     ] + [pltpu.make_async_copy(latent.at[0, :, pl.ds(u * SUB, SUB)], kv.at[base + u], lsem.at[4 + u]) for u in range(4)]
     for load in loads:
         load.start()
     vload = pltpu.make_async_copy(vu_h, vu, lsem.at[8])
     pl.when(role_a)(vload.start)
 
-    barrier = pltpu.get_barrier_semaphore()
-
-    def greet_core(i, _):
-        @pl.when(jnp.logical_not(jnp.logical_and(role_a, i == y * 4 + x)))
-        def _():
-            pl.semaphore_signal(barrier, inc=1, device_id=dev(i // 4, i % 4, z, xl), device_id_type=MESH)
-        return 0
-
-    def greet_col(i, _):
-        pl.semaphore_signal(barrier, inc=1, device_id=dev(i // 2, (i % 2) * 2 + c, z, 1 - xl), device_id_type=MESH)
-        return 0
-
-    for d in (zp, zm):
-        pl.semaphore_signal(barrier, inc=1, device_id=d, device_id_type=MESH)
-    lax.fori_loop(0, 16, greet_core, 0)
-    lax.fori_loop(0, 8, greet_col, 0)
-
+    for load in loads[4:7]:
+        load.wait()
     lab_row = labels[...]
     sub, lane = iota((S, S), 0), iota((S, S), 1)
     lab = jnp.sum(jnp.where(sub == lane, lab_row.astype(F32), 0.0), axis=1, keepdims=True).astype(jnp.int32)
@@ -107,7 +111,7 @@
     place = (iota((PL, S), 0) == rank_row * SLOTS + slot_row).astype(BF16)
     code = rank_col * SLOTS + slot_col
 
-    for load in loads:
+    for load in loads[:4] + loads[7:]:
         load.wait()
     scale = (NOPE + ROPE) ** -0.5
     nope_s = dot(place, nope[...]).astype(BF16)
@@ -153,6 +157,13 @@
             src_ref=kv.at[src], dst_ref=kv.at[dst], send_sem=kss.at[sem], recv_sem=krs.at[dst], device_id=d, device_id_type=MESH
         )
 
+    def half_copy(src, dst, half, sem, d):
+        lanes = pl.ds(half * (SUB // 2), SUB // 2)
+        return pltpu.make_async_remote_copy(
+            src_ref=kv.at[src, :, lanes], dst_ref=kv.at[dst, :, lanes], send_sem=kss.at[sem],
+            recv_sem=krs.at[dst if half == 0 else 32 + dst // 16 * 2 + dst % 2], device_id=d, device_id_type=MESH,
+        )
+
     o = jnp.where(role_a, 0, 16)
 
     def ring_own(u):
@@ -166,17 +177,32 @@
     def ring_pass(j):
         a, b = pair(j)
         out_ = [kv_copy(o + k, o + k, 12 + k, sib) for k in (a, b)]
-        if j in (2, 4):
-            out_ = [kv_copy(o + a, o + 10 + j, 6 + j, zp), kv_copy(o + b, o + 11 + j, 7 + j, zm)] + out_
+        if j == 2:
+            out_ = [kv_copy(o + a, o + 12, 8, zp), kv_copy(o + b, o + 13, 9, zm)] + out_
+        if j == 4:
+            halves_ = [(half_copy(o + a, o + 14, n, 10 + 22 * n, zp), half_copy(o + b, o + 15, n, 11 + 22 * n, zm)) for n in range(2)]
+            out_ = [*halves_[0], *halves_[1]] + out_
         return out_
+
+    def last_pass(n):
+        return [half_copy(o + 14, o + 14, n, 26 + 8 * n, sib), half_copy(o + 15, o + 15, n, 27 + 8 * n, sib)]
 
     def arrived(k):
         kv_copy(k, k, 0, sib).wait_recv()
+
+    def half_arrived(k, n):
+        half_copy(k, k, n, 0, sib).wait_recv()
 
     def ring_step(j):
         for k in pair(j):
             arrived(o + k)
         for cp in ring_pass(j):
+            cp.start()
+
+    def last_step(n):
+        half_arrived(o + 14, n)
+        half_arrived(o + 15, n)
+        for cp in last_pass(n):
             cp.start()
 
     def cross_step(u):
@@ -262,15 +288,16 @@
         mtop[rs, :] = jnp.broadcast_to(own_score, (RB, 128))
         tot[rs, :] = (iota((RB, 128), 1) == 0).astype(F32)
 
-    def attend(ka, kb, blocks):
-        def first(k):
-            s = k % 16 // 4
-            zz = (z + jnp.where(s == 1, 3, jnp.where(s == 2, 1, jnp.where(s == 3, 2, 0)))) % 4
-            return (zz * 2 + jnp.where(k < 16, xl, 1 - xl)) * SHARD + k % 4 * SUB
-
-        keys = jnp.concatenate([kv[ka], kv[kb]], axis=1)
-        lane = iota((1, CH), 1)
-        at = lane + jnp.where(lane < SUB, first(ka), first(kb) - SUB)
+    def first(k):
+        s = k % 16 // 4
+        zz = (z + jnp.where(s == 1, 3, jnp.where(s == 2, 1, jnp.where(s == 3, 2, 0)))) % 4
+        return (zz * 2 + jnp.where(k < 16, xl, 1 - xl)) * SHARD + k % 4 * SUB
+
+    def attend(ka, kb, blocks, start=0, width=SUB):
+        lanes = pl.ds(start, width)
+        keys = jnp.concatenate([kv[ka, :, lanes], kv[kb, :, lanes]], axis=1)
+        lane = iota((1, 2 * width), 1)
+        at = lane + start + jnp.where(lane < width, first(ka), first(kb) - width)
         bias = jnp.where(at < live, 0.0, NEG)
 
         def score(b):
@@ -281,7 +308,7 @@
             rs, s = pl.ds(b * RB, RB), following
             if b != blocks[-1]:
                 following = score(b + 1)
-            tiles = [s[:, 128 * j : 128 * j + 128] for j in range(CH // 128)]
+            tiles = [s[:, 128 * j : 128 * j + 128] for j in range(2 * width // 128)]
             top = mtop[rs, :]
             new_top = jnp.maximum(top, jnp.max(functools.reduce(jnp.maximum, tiles), axis=1, keepdims=True))
             shrink = jnp.exp(top - new_top)
@@ -292,9 +319,9 @@
             for j in range(4):
                 acc[j, rs, :] = acc[j, rs, :] * shrink + new[:, 128 * j : 128 * j + 128]
 
-    turns_a = {0: {2: 2, 3: 3, 4: 4}, 1: {1: 5, 4: 6}, 2: {7: 7}}
+    turns_a = {0: {2: 2, 3: 3, 4: 4}, 1: {1: 5, 4: 6}, 2: {}}
     turns_x = {0: {}, 1: {2: 0, 4: 1}, 2: {7: 2, 8: 3}}
-    turns_b = {0: {}, 1: {}, 2: {9: 2, 10: 3, 12: 4, 13: 5, 14: 6, 15: 7}}
+    turns_b = {0: {}, 1: {}, 2: {9: 2, 10: 3, 12: 4, 13: 5, 14: 6}}
 
     def step(loop, blocks, i, _):
         j = i % 8
@@ -311,6 +338,11 @@
             for at, k in turns_a[loop].items():
                 pl.when(i == at)(functools.partial(ring_step, k))
             if loop == 2:
+
+                @pl.when(i == 7)
+                def _():
+                    last_step(0)
+                    last_step(1)
 
                 pl.when(i == 5)(halves[1].start)
                 pl.when(i == 8)(halves[0].start)
@@ -325,7 +357,13 @@
             if loop == 0:
                 both()
             if loop == 2:
-                pl.when(i < 8)(both)
+                pl.when(i < 7)(both)
+
+                @pl.when(i == 7)
+                def _():
+                    for n in range(2):
+                        half_arrived(14, n)
+                        half_arrived(15, n)
 
         attend(ka, kb, blocks)
         return 0
@@ -337,7 +375,16 @@
     open_block(1)
     open_block(2)
     lax.fori_loop(0, EARLY, functools.partial(step, 1, (1, 2)), 0)
-    lax.fori_loop(EARLY, 16, functools.partial(step, 2, (0, 1, 2)), 0)
+    lax.fori_loop(EARLY, 15, functools.partial(step, 2, (0, 1, 2)), 0)
+    for n in range(2):
+        pl.when(jnp.logical_not(role_a))(functools.partial(last_step, n))
+
+        @pl.when(role_a)
+        def _():
+            half_arrived(30, n)
+            half_arrived(31, n)
+
+        attend(30, 31, (0, 1, 2), n * (SUB // 2), SUB // 2)
 
     @pl.when(role_a)
     def _():
@@ -385,8 +432,11 @@
     for u in range(4):
         for cp in ring_own(u):
             cp.wait_send()
-    for j in range(2, 8):
+    for j in range(2, 7):
         for cp in ring_pass(j):
+            cp.wait_send()
+    for n in range(2):
+        for cp in last_pass(n):
             cp.wait_send()
 
     def all_wait(i, _):
@@ -416,14 +466,17 @@
 
 
 def shards(latent_cache, query_nope, query_rope, new_latent, key_up, value_up, prompt_owner, prompt_length, sample_prompt):
-    hbm, smem, vmem = (pl.BlockSpec(memory_space=m) for m in (pl.ANY, pltpu.SMEM, pltpu.VMEM))
+    hbm, vmem = (pl.BlockSpec(memory_space=m) for m in (pl.ANY, pltpu.VMEM))
     dma = pltpu.SemaphoreType.DMA
     return pl.pallas_call(
         kernel,
         out_shape=pltpu.VMEM(query_nope.shape, BF16),
-        in_specs=[hbm] * 6 + [smem] * 2 + [vmem],
+        in_specs=[hbm] * 9,
         out_specs=vmem,
         scratch_shapes=[
+            pltpu.VMEM((1, S), jnp.int32),
+            pltpu.SMEM((SLOTS,), jnp.int32),
+            pltpu.SMEM((SLOTS,), jnp.int32),
             pltpu.VMEM(query_nope.shape, BF16),
             pltpu.VMEM(query_rope.shape, BF16),
             pltpu.VMEM(new_latent.shape, BF16),
@@ -439,7 +492,7 @@
             pltpu.VMEM((CAP, RB, DV), BF16),
             pltpu.VMEM((CAP, RB, DV), BF16),
             pltpu.VMEM((HL * S, ROWS), BF16),
-            dma((9,)), dma((2 * SLOTS,)), dma((2 * SLOTS,)), dma((32,)), dma((32,)),
+            dma((12,)), dma((2 * SLOTS,)), dma((2 * SLOTS,)), dma((36,)), dma((36,)),
             dma((2,)), dma((2,)), dma((SLOTS,)), dma((SLOTS,)),
         ],
         compiler_params=pltpu.CompilerParams(collective_id=0, has_side_effects=True, vmem_limit_bytes=56 << 20),

time: 62 us -> 61 us (0.984)
  Pallas kernels: 61.2 us -> 60.2 us
    pallas_call x1, Pallas kernels: 61.2 us -> 60.2 us  [shards(): pl.pallas_call(kernel, out_shape=pltpu.VMEM(query_nope.shape, BF16), in_s...]
where the time goes in v4:
time: 61 us; the launch traced here: 60.9 us
  Pallas kernels  60.2 us (99%)
  local copies, waits for them, and re-layouts  0.64 us (1%)
    pallas_call x1, Pallas kernels, shards(): pl.pallas_call(kernel, out_shape=pltpu.VMEM(query_nope.shape, BF16), in_s...  60.2 us

profile of v4, /device:TPU:1, one launch (start us, length us, event | category | flops | bytes accessed | tf_op | source)
XLA Modules:
  0.0 60.9 jit_solution(1729815036722646392)
XLA Ops:
  0.0 60.2 %shard_map.91 = bf16[24,2048]{1,0:T(8,128)(2,1)S(1)} custom-call(bf16[1,576,1024]{2,1,0:T(8,128)(2,1)} %bitcast.2, bf16[24,2048]{1,0:T(8,128)(2,1)} %nope_h.1, bf16[24,1024]{1,0:T(8,128)(2,1)} %rope_h.1, bf16[24,576]{1,0:T(8,128)(2,1)} %new_h.1, bf16[16,128,512]{2,1,0:T(8,128)(2,1)} %ku_h.1, bf16[16,512,128]{2,1,0:T(8,128)(2,1)} %vu_h.1, s32[16]{0:T(128)} %owner_h.1, ...), custom_call_target="tpu_custom_call" | custom-call | flops 17179869184 | bytes 8388608 | tf_op jit(solution)/shard_map/pallas_call | solution.py:471
  60.2 0.6 %copy.11 = bf16[24,2048]{1,0:T(8,128)(2,1)} copy(bf16[24,2048]{1,0:T(8,128)(2,1)S(1)} %shard_map.91) | data formatting | bytes 196608

commit v5 on v4

--- a/solution.py
+++ b/solution.py
@@ -135,7 +135,7 @@
         else:
             piece = jnp.zeros_like(mine)
         stage[4, rows, :] = jnp.where(low, mine, piece)
-    for h in range(HL // 2):
+    for h in range(HL // 4):
         absorb(h)
 
     places = (pl.ds(0, 1), pl.ds(1, 2))
@@ -222,7 +222,7 @@
             by_part[u ^ 1][1].start()
             by_part[u][2].start()
 
-    for h in range(HL // 2, HL):
+    for h in range(HL // 4, HL):
         absorb(h)
     for j in range(5):
         qsend[:, :, pl.ds(128 * j, 128)] = stage[j].astype(BF16).reshape(CAP, RB, 128)
@@ -300,14 +300,10 @@
         at = lane + start + jnp.where(lane < width, first(ka), first(kb) - width)
         bias = jnp.where(at < live, 0.0, NEG)
 
-        def score(b):
-            return dot(q[b, :, pl.ds(0, KW)], keys) + bias
-
-        following = score(blocks[0])
-        for b in blocks:
-            rs, s = pl.ds(b * RB, RB), following
-            if b != blocks[-1]:
-                following = score(b + 1)
+        scores = [dot(q[b, :, pl.ds(0, KW)], keys) + bias for b in blocks]
+        shrinks, weights_bf = [], []
+        for b, s in zip(blocks, scores):
+            rs = pl.ds(b * RB, RB)
             tiles = [s[:, 128 * j : 128 * j + 128] for j in range(2 * width // 128)]
             top = mtop[rs, :]
             new_top = jnp.maximum(top, jnp.max(functools.reduce(jnp.maximum, tiles), axis=1, keepdims=True))
@@ -315,7 +311,11 @@
             weights = [jnp.exp(a - new_top) for a in tiles]
             tot[rs, :] = tot[rs, :] * shrink + functools.reduce(jnp.add, weights)
             mtop[rs, :] = new_top
-            new = dot_nt(jnp.concatenate([a.astype(BF16) for a in weights], axis=1), keys[:LAT])
+            shrinks.append(shrink)
+            weights_bf.append(jnp.concatenate([a.astype(BF16) for a in weights], axis=1))
+        for b, shrink, w in zip(blocks, shrinks, weights_bf):
+            rs = pl.ds(b * RB, RB)
+            new = dot_nt(w, keys[:LAT])
             for j in range(4):
                 acc[j, rs, :] = acc[j, rs, :] * shrink + new[:, 128 * j : 128 * j + 128]
 
@@ -410,14 +410,14 @@
 
     own_o = pltpu.make_async_copy(osend.at[:, block(r)], orecv.at[:, block(r)], ors.at[r])
 
-    def o_send(i, _):
-        g = (r + i) % SLOTS
-        kept = jnp.logical_and(role_a, i == 0)
-        pl.when(kept)(own_o.start)
-        pl.when(jnp.logical_not(kept))(lambda: o_copy(g).start())
-        return 0
-
-    lax.fori_loop(0, SLOTS, o_send, 0)
+    for iy in (2, 1, 3, 0):
+        for ix, ic in ((1, 0), (1, 1), (0, 0), (0, 1)):
+            g = ((y + iy) % 4 * 2 + (xh + ix) % 2) * 2 + (c + ic) % 2
+            if iy + ix + ic:
+                o_copy(g).start()
+            else:
+                pl.when(role_a)(own_o.start)
+                pl.when(jnp.logical_not(role_a))(o_copy(g).start)
 
     @pl.when(role_a)
     def _():

time: 61 us -> 60.4 us (level)
  no operation moved by 1% of the time
where the time goes in v5:
time: 60.4 us; the launch traced here: 60.3 us
  Pallas kernels  59.6 us (99%)
  local copies, waits for them, and re-layouts  0.64 us (1%)
    pallas_call x1, Pallas kernels, shards(): pl.pallas_call(kernel, out_shape=pltpu.VMEM(query_nope.shape, BF16), in_s...  59.6 us

profile of v5, /device:TPU:1, one launch (start us, length us, event | category | flops | bytes accessed | tf_op | source)
XLA Modules:
  0.0 60.3 jit_solution(10673073095517612643)
XLA Ops:
  0.0 59.6 %shard_map.91 = bf16[24,2048]{1,0:T(8,128)(2,1)S(1)} custom-call(bf16[1,576,1024]{2,1,0:T(8,128)(2,1)} %bitcast.2, bf16[24,2048]{1,0:T(8,128)(2,1)} %nope_h.1, bf16[24,1024]{1,0:T(8,128)(2,1)} %rope_h.1, bf16[24,576]{1,0:T(8,128)(2,1)} %new_h.1, bf16[16,128,512]{2,1,0:T(8,128)(2,1)} %ku_h.1, bf16[16,512,128]{2,1,0:T(8,128)(2,1)} %vu_h.1, s32[16]{0:T(128)} %owner_h.1, ...), custom_call_target="tpu_custom_call" | custom-call | flops 17179869184 | bytes 8388608 | tf_op jit(solution)/shard_map/pallas_call | solution.py:471
  59.6 0.6 %copy.11 = bf16[24,2048]{1,0:T(8,128)(2,1)} copy(bf16[24,2048]{1,0:T(8,128)(2,1)S(1)} %shard_map.91) | data formatting | bytes 196608

commit v6 on v5

--- a/solution.py
+++ b/solution.py
@@ -176,13 +176,14 @@
 
     def ring_pass(j):
         a, b = pair(j)
-        out_ = [kv_copy(o + k, o + k, 12 + k, sib) for k in (a, b)]
+        on_a, on_b = ([kv_copy(o + k, o + k, 12 + k, sib)] for k in (a, b))
         if j == 2:
-            out_ = [kv_copy(o + a, o + 12, 8, zp), kv_copy(o + b, o + 13, 9, zm)] + out_
+            on_a = [kv_copy(o + a, o + 12, 8, zp)] + on_a
+            on_b = [kv_copy(o + b, o + 13, 9, zm)] + on_b
         if j == 4:
-            halves_ = [(half_copy(o + a, o + 14, n, 10 + 22 * n, zp), half_copy(o + b, o + 15, n, 11 + 22 * n, zm)) for n in range(2)]
-            out_ = [*halves_[0], *halves_[1]] + out_
-        return out_
+            on_a = [half_copy(o + a, o + 14, n, 10 + 22 * n, zp) for n in range(2)] + on_a
+            on_b = [half_copy(o + b, o + 15, n, 11 + 22 * n, zm) for n in range(2)] + on_b
+        return on_a, on_b
 
     def last_pass(n):
         return [half_copy(o + 14, o + 14, n, 26 + 8 * n, sib), half_copy(o + 15, o + 15, n, 27 + 8 * n, sib)]
@@ -194,15 +195,14 @@
         half_copy(k, k, n, 0, sib).wait_recv()
 
     def ring_step(j):
-        for k in pair(j):
+        for k, onward in zip(pair(j), ring_pass(j)):
             arrived(o + k)
-        for cp in ring_pass(j):
-            cp.start()
+            for cp in onward:
+                cp.start()
 
     def last_step(n):
-        half_arrived(o + 14, n)
-        half_arrived(o + 15, n)
-        for cp in last_pass(n):
+        for k, cp in zip((14, 15), last_pass(n)):
+            half_arrived(o + k, n)
             cp.start()
 
     def cross_step(u):
@@ -225,7 +225,7 @@
     for h in range(HL // 4, HL):
         absorb(h)
     for j in range(5):
-        qsend[:, :, pl.ds(128 * j, 128)] = stage[j].astype(BF16).reshape(CAP, RB, 128)
+        qsend[:, :, pl.ds(128 * j, 128)] = stage[j, pl.ds(0, ROWS), :].astype(BF16).reshape(CAP, RB, 128)
 
     def q_send(n, i, _):
         s = swap(slot, i)
@@ -400,7 +400,7 @@
         share = 1.0 / jnp.sum(tot[rows, :], axis=1, keepdims=True)
         mean = jnp.concatenate([acc[j, rows, :] * share for j in range(4)], axis=1).astype(BF16)
         stage[0, rows, :] = dot(mean, vu[h])
-    osend[...] = stage[0].astype(BF16).reshape(CAP, RB, DV)
+    osend[...] = stage[0, pl.ds(0, ROWS), :].astype(BF16).reshape(CAP, RB, DV)
 
     def o_copy(g):
         return pltpu.make_async_remote_copy(
@@ -433,8 +433,9 @@
         for cp in ring_own(u):
             cp.wait_send()
     for j in range(2, 7):
-        for cp in ring_pass(j):
-            cp.wait_send()
+        for onward in ring_pass(j):
+            for cp in onward:
+                cp.wait_send()
     for n in range(2):
         for cp in last_pass(n):
             cp.wait_send()
@@ -483,12 +484,12 @@
             pltpu.VMEM(key_up.shape, BF16),
             pltpu.VMEM(value_up.shape, BF16),
             pltpu.VMEM((36, KW, SUB), BF16),
-            pltpu.VMEM((5, ROWS, 128), F32),
+            pltpu.VMEM((5, ROWS + HL, 128), F32),
             pltpu.VMEM((CAP, RB, QW), BF16),
             pltpu.VMEM((CAP, RB, QW), BF16),
             pltpu.VMEM((ROWS, 128), F32),
-            pltpu.VMEM((ROWS, 128), F32),
-            pltpu.VMEM((4, ROWS, 128), F32),
+            pltpu.VMEM((ROWS + HL, 128), F32),
+            pltpu.VMEM((4, ROWS + HL, 128), F32),
             pltpu.VMEM((CAP, RB, DV), BF16),
             pltpu.VMEM((CAP, RB, DV), BF16),
             pltpu.VMEM((HL * S, ROWS), BF16),

time: 60.4 us -> 60.4 us (level)
  no operation moved by 1% of the time
where the time goes in v6:
time: 60.4 us; the launch traced here: 60.3 us
  Pallas kernels  59.6 us (99%)
  local copies, waits for them, and re-layouts  0.64 us (1%)
    pallas_call x1, Pallas kernels, shards(): pl.pallas_call(kernel, out_shape=pltpu.VMEM(query_nope.shape, BF16), in_s...  59.6 us

profile of v6, /device:TPU:1, one launch (start us, length us, event | category | flops | bytes accessed | tf_op | source)
XLA Modules:
  0.0 60.3 jit_solution(4043389145453690730)
XLA Ops:
  0.0 59.6 %shard_map.91 = bf16[24,2048]{1,0:T(8,128)(2,1)S(1)} custom-call(bf16[1,576,1024]{2,1,0:T(8,128)(2,1)} %bitcast.2, bf16[24,2048]{1,0:T(8,128)(2,1)} %nope_h.1, bf16[24,1024]{1,0:T(8,128)(2,1)} %rope_h.1, bf16[24,576]{1,0:T(8,128)(2,1)} %new_h.1, bf16[16,128,512]{2,1,0:T(8,128)(2,1)} %ku_h.1, bf16[16,512,128]{2,1,0:T(8,128)(2,1)} %vu_h.1, s32[16]{0:T(128)} %owner_h.1, ...), custom_call_target="tpu_custom_call" | custom-call | flops 17179869184 | bytes 8388608 | tf_op jit(solution)/shard_map/pallas_call | solution.py:472
  59.6 0.6 %copy.11 = bf16[24,2048]{1,0:T(8,128)(2,1)} copy(bf16[24,2048]{1,0:T(8,128)(2,1)S(1)} %shard_map.91) | data formatting | bytes 196608

commit v7 on v6

--- a/solution.py
+++ b/solution.py
@@ -227,15 +227,14 @@
     for j in range(5):
         qsend[:, :, pl.ds(128 * j, 128)] = stage[j, pl.ds(0, ROWS), :].astype(BF16).reshape(CAP, RB, 128)
 
-    def q_send(n, i, _):
-        s = swap(slot, i)
-        kept = jnp.logical_and(role_a, i == 0)
-        pl.when(kept)(lambda: own_q(n).start())
-        pl.when(jnp.logical_not(kept))(lambda: q_copy(n, s, q_dev(s)).start())
-        return 0
-
     for n in range(2):
-        lax.fori_loop(0, SLOTS, functools.partial(q_send, n), 0)
+        for i in range(SLOTS):
+            s = swap(slot, i)
+            if i:
+                q_copy(n, s, q_dev(s)).start()
+            else:
+                pl.when(role_a)(own_q(n).start)
+                pl.when(jnp.logical_not(role_a))(q_copy(n, s, q_dev(s)).start)
 
     @pl.when(jnp.logical_not(role_a))
     def _():

time: 60.4 us -> 60.4 us (level)
  no operation moved by 1% of the time
where the time goes in v7:
time: 60.4 us; the launch traced here: 60.3 us
  Pallas kernels  59.6 us (99%)
  local copies, waits for them, and re-layouts  0.64 us (1%)
    pallas_call x1, Pallas kernels, shards(): pl.pallas_call(kernel, out_shape=pltpu.VMEM(query_nope.shape, BF16), in_s...  59.6 us

profile of v7, /device:TPU:1, one launch (start us, length us, event | category | flops | bytes accessed | tf_op | source)
XLA Modules:
  0.0 60.3 jit_solution(3681562474344178315)
XLA Ops:
  0.0 59.6 %shard_map.91 = bf16[24,2048]{1,0:T(8,128)(2,1)S(1)} custom-call(bf16[1,576,1024]{2,1,0:T(8,128)(2,1)} %bitcast.2, bf16[24,2048]{1,0:T(8,128)(2,1)} %nope_h.1, bf16[24,1024]{1,0:T(8,128)(2,1)} %rope_h.1, bf16[24,576]{1,0:T(8,128)(2,1)} %new_h.1, bf16[16,128,512]{2,1,0:T(8,128)(2,1)} %ku_h.1, bf16[16,512,128]{2,1,0:T(8,128)(2,1)} %vu_h.1, s32[16]{0:T(128)} %owner_h.1, ...), custom_call_target="tpu_custom_call" | custom-call | flops 17179869184 | bytes 8388608 | tf_op jit(solution)/shard_map/pallas_call | solution.py:471
  59.6 0.6 %copy.11 = bf16[24,2048]{1,0:T(8,128)(2,1)} copy(bf16[24,2048]{1,0:T(8,128)(2,1)S(1)} %shard_map.91) | data formatting | bytes 196608
